TPU v7x, 256 devices: a whole 4x4x8 slice. The times are simulated.
256 devices in a mesh: seq: 64 (over z, x, y_hi), heads: 4 (over y_lo, core).
Axes of the slice: x: 4, y: 4 (y_hi: 2, y_lo: 2; y = y_hi * 2 + y_lo), z: 8, core: 2. Of those that a mesh axis runs over, the one named last changes fastest.
Arguments:
- query: bfloat16 [16384, 1024], P('seq', 'heads'), may hold values from -6 to 6
- key_rows: bfloat16 [16384, 128], P('seq'), may hold values from -6 to 6
- head_value_rows: bfloat16 [16384, 128], P('seq'), may hold values from -6 to 6
- output: bfloat16 [16384, 1024], P('seq', 'heads'), may hold values from -6 to 6
- out_grad: bfloat16 [16384, 1024], P('seq', 'heads'), may hold values from -0.59765625 to 0.59765625
- logsumexp: float32 [8, 16384], P('heads', 'seq'), as said below
- block_pos: int32 [128], P('seq'), may hold values from 0 to 127, as said below
Outputs:
- query_grad: bfloat16 [16384, 1024], P('seq', 'heads')
- key_grad: bfloat16 [16384, 128], P('seq')
- value_grad: bfloat16 [16384, 128], P('seq')
Inputs may be any that keep to these rules, and one draw needn't show every extreme that they name: `block_pos`: a permutation of the half-block numbers in which stored half-blocks 2 d and 2 d + 1 hold sequence half-blocks b and 127 - b for some b < 64. `logsumexp`: an input offset near log(1.65 (pos + 1)) of the row's sequence position, not recomputed from the scores.
All inputs are finite; a program needn't handle non-finite values.
Results may differ from a plain program's by a relative error of at most 0.0052.
Values may be sent and summed in bfloat16 or wider, within the bound.
No kernel may reach another device: no remote copies, remote signals or barrier semaphores. Data moves between devices by JAX's collectives and lax.ppermute only.
A program may use at most 64 MiB of HBM per device.

v0:
```python
import math

import jax
import jax.numpy as jnp
from jax import lax
from jax.sharding import PartitionSpec as P


def shifted(block, axis, distance):
    devices = range(lax.axis_size(axis))
    route = [((i - distance) % len(devices), i) for i in devices]
    return lax.ppermute(block, axis, route)


def shards(query, key_rows, head_value_rows, output, out_grad, logsumexp, block_pos):
    tok = query.shape[0]
    half = tok // 2
    hdim = key_rows.shape[1]
    heads = query.shape[1] // hdim
    scale = 1.0 / math.sqrt(hdim)
    seq_count = lax.axis_size("seq")
    query3 = query.reshape(tok, heads, hdim)
    grad3 = out_grad.reshape(tok, heads, hdim)
    delta = jnp.sum(
        (output.astype(jnp.float32) * out_grad.astype(jnp.float32)).reshape(tok, heads, hdim),
        axis=-1,
    ).T
    qpos = (block_pos[:, None] * half + jnp.arange(half, dtype=jnp.int32)[None, :]).reshape(tok)

    def make_tile(query_place):
        qrows = query3[query_place * half : (query_place + 1) * half]
        grows = grad3[query_place * half : (query_place + 1) * half]
        drows = delta[:, query_place * half : (query_place + 1) * half]
        lrows = logsumexp[:, query_place * half : (query_place + 1) * half]
        prows = qpos[query_place * half : (query_place + 1) * half]

        def tile_terms(key_block, value_block, key_positions):
            scores = (
                jnp.einsum("thd,kd->htk", qrows, key_block, preferred_element_type=jnp.float32)
                * scale
            )
            allowed = key_positions[None, None, :] <= prows[None, :, None]
            probs = jnp.where(allowed, jnp.exp(scores - lrows[:, :, None]), 0.0)
            value_add = jnp.einsum(
                "htk,thd->kd", probs.astype(jnp.bfloat16), grows, preferred_element_type=jnp.float32
            )
            dprobs = jnp.einsum(
                "thd,kd->htk", grows, value_block, preferred_element_type=jnp.float32
            )
            dscores = (probs * (dprobs - drows[:, :, None])).astype(jnp.bfloat16)
            query_add = jnp.einsum(
                "htk,kd->thd", dscores, key_block, preferred_element_type=jnp.float32
            )
            key_add = jnp.einsum("htk,thd->kd", dscores, qrows, preferred_element_type=jnp.float32)
            return (query_add, key_add, value_add)

        def tile(key_block, value_block, key_positions):
            return tile_terms(key_block, value_block, key_positions)

        return tile

    tile_list = [make_tile(0), make_tile(1)]

    def add_contribution(key_block, value_block, key_positions):
        query_pieces = []
        key_pieces = []
        value_pieces = []
        for kslot in range(2):
            key_portion = key_block[kslot * half : (kslot + 1) * half]
            value_portion = value_block[kslot * half : (kslot + 1) * half]
            probs_portion = key_positions[kslot * half : (kslot + 1) * half]
            key_sum = jnp.zeros((half, hdim), jnp.float32)
            value_grand_sum = jnp.zeros((half, hdim), jnp.float32)
            for query_place in range(2):
                query_increment, key_increment, value_increment = tile_list[query_place](
                    key_portion, value_portion, probs_portion
                )
                key_sum = key_sum + key_increment
                value_grand_sum = value_grand_sum + value_increment
                if kslot == 0:
                    query_pieces.append(query_increment)
                else:
                    query_pieces[query_place] = query_pieces[query_place] + query_increment
            key_pieces.append(key_sum)
            value_pieces.append(value_grand_sum)
        return (
            jnp.concatenate(query_pieces, 0),
            jnp.concatenate(key_pieces, 0),
            jnp.concatenate(value_pieces, 0),
        )

    query_acc = jnp.zeros((tok, heads, hdim), jnp.float32)

    def loop_step(index, carry):
        key_block, value_block, key_positions, key_grad_running, value_grad_running, qacc = carry
        next_k, next_v, next_p = shifted((key_block, value_block, key_positions), "seq", 1)
        query_increment, key_increment, value_increment = add_contribution(
            key_block, value_block, key_positions
        )
        key_grad_running, value_grad_running = shifted(
            (key_grad_running + key_increment, value_grad_running + value_increment), "seq", 1
        )
        return (
            next_k,
            next_v,
            next_p,
            key_grad_running,
            value_grad_running,
            qacc + query_increment,
        )

    zero_full = jnp.zeros((tok, hdim), jnp.float32)
    start = (key_rows, head_value_rows, qpos, zero_full, zero_full, query_acc)
    key_block, value_block, key_positions, key_grad_running, value_grad_running, query_acc = (
        lax.fori_loop(0, seq_count - 1, loop_step, start)
    )
    query_increment, key_increment, value_increment = add_contribution(
        key_block, value_block, key_positions
    )
    query_acc = query_acc + query_increment
    key_running_sum, value_running_sum = shifted(
        (key_grad_running + key_increment, value_grad_running + value_increment), "seq", 1
    )
    key_total, value_total = lax.psum((key_running_sum, value_running_sum), "heads")
    query_grad = (query_acc * scale).reshape(tok, heads * hdim).astype(jnp.bfloat16)
    return (query_grad, (key_total * scale).astype(jnp.bfloat16), value_total.astype(jnp.bfloat16))


def solution(mesh):
    in_specs = (
        P("seq", "heads"),
        P("seq", None),
        P("seq", None),
        P("seq", "heads"),
        P("seq", "heads"),
        P("heads", "seq"),
        P("seq"),
    )
    out_specs = (P("seq", "heads"), P("seq", None), P("seq", None))
    return jax.shard_map(shards, mesh=mesh, in_specs=in_specs, out_specs=out_specs, check_vma=False)
```

profile of v0, /device:TPU:1, one launch (start us, length us, event | category | flops | bytes accessed | tf_op | source)
XLA Modules:
  0.0 1364.0 jit_solution(1238822549381637441)
XLA Ops:
  12.6 1153.6 %while.21 = (s32[]{:T(128)}, bf16[256,128]{1,0:T(8,128)(2,1)S(1)}, bf16[256,128]{1,0:T(8,128)(2,1)S(1)}, s32[256]{0:T(256)S(1)}, f32[256,128]{1,0:T(8,128)S(1)},...) while((s32[]{:T(128)}, bf16[256,128]{1,0:T(8,128)(2,1)S(1)}, ...), condition=%wide.region_2.3_spmd.clone, body=%wide.region_1.2_spmd.clone.sunk | while | flops 169213952 | bytes 8931711 | solution.py:115
  48.4 4.7 collective-permute-done.3
  66.9 5.1 collective-permute-done.3
  83.6 6.9 collective-permute-done.3
  102.6 5.7 collective-permute-done.3
  121.8 5.7 collective-permute-done.3
  139.9 4.5 collective-permute-done.3
  155.9 5.4 collective-permute-done.3
  161.4 4.9 collective-permute-start
  177.4 5.7 collective-permute-done.3
  199.0 6.5 collective-permute-done.3
  235.3 5.2 collective-permute-done.3
  269.0 5.8 collective-permute-done.3
  276.5 4.4 collective-permute-start.4
  287.2 4.6 collective-permute-done.3
  306.6 5.2 collective-permute-done.3
  323.1 5.2 collective-permute-done.3
  340.4 5.1 collective-permute-done.3
  371.7 4.5 collective-permute-done.4
  376.2 5.7 collective-permute-done.3
  395.7 5.7 collective-permute-done.3
  428.5 5.3 collective-permute-done.3
  439.2 4.7 collective-permute-start.4
  448.8 6.0 collective-permute-done.3
  468.0 5.7 collective-permute-done.3
  473.8 4.4 collective-permute-start
  479.7 4.7 collective-permute-start.4
  490.9 4.4 collective-permute-done.3
  525.3 6.5 collective-permute-done.3
  547.2 4.4 collective-permute-start
  562.8 5.7 collective-permute-done.3
  598.6 5.7 collective-permute-done.3
  631.5 5.1 collective-permute-done.3
  666.8 6.5 collective-permute-done.3
  687.2 5.0 collective-permute-done.3
  719.5 4.6 collective-permute-done.3
  739.3 6.4 collective-permute-done.3
  757.1 5.2 collective-permute-done.3
  762.7 5.6 collective-permute-start
  779.4 7.3 collective-permute-done.3
  798.0 4.9 collective-permute-done.3
  805.7 4.7 collective-permute-start.4
  815.8 5.5 collective-permute-done.3
  832.7 4.5 collective-permute-done.3
  852.4 5.7 collective-permute-done.3
  875.0 5.1 collective-permute-start
  891.2 5.7 collective-permute-done.3
  923.8 4.5 collective-permute-done.3
  940.4 5.7 collective-permute-done.3
  958.1 5.7 collective-permute-done.3
  963.9 4.9 collective-permute-start
  970.4 4.7 collective-permute-start.4
  980.8 5.2 collective-permute-done.3
  1031.0 5.4 collective-permute-done.3
  1055.4 5.5 collective-permute-start
  1072.3 5.7 collective-permute-done.3
  1090.4 4.7 collective-permute-done.3
  1107.0 5.2 collective-permute-done.3
  1127.5 7.8 collective-permute-start
  1136.7 4.7 collective-permute-start.4
  1146.3 6.0 collective-permute-done.3
  1171.0 8.1 collective-permute-done.5
  1180.5 151.3 %all-reduce.4 = bf16[256,128]{1,0:T(8,128)(2,1)} all-reduce(f32[256,128]{1,0:T(8,128)S(1)} %collective-permute-done.6), channel_id=1, replica_groups=mesh['seq'=64,'heads'=4] {'heads'}, use_global_device_ids=true, to_apply=%region_4.5 | all-reduce | flops 32768 | bytes 196608 | tf_op jit(solution)/shard_map/psum | solution.py:124
  1331.7 23.9 %all-reduce.3.cloned.1.call-done = f32[256,128]{1,0:T(8,128)} async-done(((f32[256,128]{1,0:T(8,128)}), f32[256,128]{1,0:T(8,128)}) %all-reduce.3.cloned.1.call-update) | async-done | bytes 131088 | tf_op jit(solution)/shard_map/psum | solution.py:124
  (2406 shorter events, 833.5 us)
Async XLA Ops:
  7.2 1348.5 %all-reduce.3.cloned.1.call-start = ((), (), s32[]{:S(2)}) async-start(), calls=%async_computation | async-start | bytes 262144 | tf_op jit(solution)/shard_map/psum | solution.py:124
  12.6 15.4 %collective-permute-start.2 = (s32[256]{0:T(256)S(1)}, s32[256]{0:T(256)S(1)}, u32[]{:S(2)}, u32[]{:S(2)}) collective-permute-start(s32[256]{0:T(256)S(1)} %copy.128), channel_id=1, source_target_pairs={{252,0},{0,4},{4,8},{8,12},{12,16},{16,20},{20,24},{24,28},{28,32}... | collective-permute-start | bytes 3080 | tf_op jit(solution)/shard_map/while/body/eval_jaxpr/ppermute | solution.py:12
  16.3 11.7 collective-permute-start.1
  41.8 11.3 collective-permute-start.3
  161.3 13.2 collective-permute-start.2
  161.3 13.2 collective-permute-start.1
  161.4 13.1 collective-permute-start
  183.0 12.2 collective-permute-start.2
  183.0 12.2 collective-permute-start.1
  183.2 12.1 collective-permute-start
  194.2 11.2 collective-permute-start.3
  207.2 11.6 collective-permute-start.4
  220.7 11.8 collective-permute-start.2
  220.7 11.8 collective-permute-start.1
  220.9 11.7 collective-permute-start
  291.9 11.3 collective-permute-start.2
  291.9 11.3 collective-permute-start.1
  347.2 11.6 collective-permute-start.4
  370.7 11.2 collective-permute-start.3
  381.9 11.5 collective-permute-start.2
  381.9 11.5 collective-permute-start.1
  382.0 11.4 collective-permute-start
  433.8 12.5 collective-permute-start.2
  433.8 12.5 collective-permute-start.1
  433.9 12.4 collective-permute-start
  473.7 13.1 collective-permute-start.2
  473.7 13.1 collective-permute-start.1
  473.8 13.0 collective-permute-start
  520.6 11.2 collective-permute-start.3
  533.5 11.6 collective-permute-start.4
  547.1 13.4 collective-permute-start.2
  547.1 13.4 collective-permute-start.1
  547.2 13.3 collective-permute-start
  583.9 11.8 collective-permute-start.2
  583.9 11.8 collective-permute-start.1
  584.0 11.7 collective-permute-start
  662.0 11.3 collective-permute-start.3
  693.8 11.9 collective-permute-start.4
  724.1 12.8 collective-permute-start.2
  724.2 12.8 collective-permute-start.1
  724.3 12.7 collective-permute-start
  762.3 14.2 %collective-permute-start.2 = (s32[256]{0:T(256)S(1)}, s32[256]{0:T(256)S(1)}, u32[]{:S(2)}, u32[]{:S(2)}) collective-permute-start(s32[256]{0:T(256)S(1)} %copy.128), channel_id=1, source_target_pairs={{252,0},{0,4},{4,8},{8,12},{12,16},{16,20},{20,24},{24,28},{28,32}... | collective-permute-start | bytes 3080 | tf_op jit(solution)/shard_map/while/body/eval_jaxpr/ppermute | solution.py:12
  762.3 14.2 %collective-permute-start.1 = (bf16[256,128]{1,0:T(8,128)(2,1)S(1)}, bf16[256,128]{1,0:T(8,128)(2,1)S(1)}, u32[]{:S(2)}, u32[]{:S(2)}) collective-permute-start(bf16[256,128]{1,0:T(8,128)(2,1)S(1)} %copy.127), channel_id=1, source_target_pairs={{252,0},{0,4},{4,8},{8,12},{12,16},{16,20},{20,24},{24,28},{28,32}... | collective-permute-start | bytes 196616 | tf_op jit(solution)/shard_map/while/body/eval_jaxpr/ppermute | solution.py:12
  762.7 13.8 %collective-permute-start = (bf16[256,128]{1,0:T(8,128)(2,1)S(1)}, bf16[256,128]{1,0:T(8,128)(2,1)S(1)}, u32[]{:S(2)}, u32[]{:S(2)}) collective-permute-start(bf16[256,128]{1,0:T(8,128)(2,1)S(1)} %copy.126), channel_id=1, source_target_pairs={{252,0},{0,4},{4,8},{8,12},{12,16},{16,20},{20,24},{24,28},{28,32}... | collective-permute-start | bytes 196616 | tf_op jit(solution)/shard_map/while/body/eval_jaxpr/ppermute | solution.py:12
  837.2 12.4 collective-permute-start.2
  837.2 12.4 collective-permute-start.1
  837.3 12.3 collective-permute-start
  874.6 14.3 %collective-permute-start.2 = (s32[256]{0:T(256)S(1)}, s32[256]{0:T(256)S(1)}, u32[]{:S(2)}, u32[]{:S(2)}) collective-permute-start(s32[256]{0:T(256)S(1)} %copy.128), channel_id=1, source_target_pairs={{252,0},{0,4},{4,8},{8,12},{12,16},{16,20},{20,24},{24,28},{28,32}... | collective-permute-start | bytes 3080 | tf_op jit(solution)/shard_map/while/body/eval_jaxpr/ppermute | solution.py:12
  874.6 14.3 %collective-permute-start.1 = (bf16[256,128]{1,0:T(8,128)(2,1)S(1)}, bf16[256,128]{1,0:T(8,128)(2,1)S(1)}, u32[]{:S(2)}, u32[]{:S(2)}) collective-permute-start(bf16[256,128]{1,0:T(8,128)(2,1)S(1)} %copy.127), channel_id=1, source_target_pairs={{252,0},{0,4},{4,8},{8,12},{12,16},{16,20},{20,24},{24,28},{28,32}... | collective-permute-start | bytes 196616 | tf_op jit(solution)/shard_map/while/body/eval_jaxpr/ppermute | solution.py:12
  875.0 13.9 %collective-permute-start = (bf16[256,128]{1,0:T(8,128)(2,1)S(1)}, bf16[256,128]{1,0:T(8,128)(2,1)S(1)}, u32[]{:S(2)}, u32[]{:S(2)}) collective-permute-start(bf16[256,128]{1,0:T(8,128)(2,1)S(1)} %copy.126), channel_id=1, source_target_pairs={{252,0},{0,4},{4,8},{8,12},{12,16},{16,20},{20,24},{24,28},{28,32}... | collective-permute-start | bytes 196616 | tf_op jit(solution)/shard_map/while/body/eval_jaxpr/ppermute | solution.py:12
  963.8 13.6 collective-permute-start.2
  963.8 13.6 collective-permute-start.1
  963.9 13.5 collective-permute-start
  1002.4 12.0 collective-permute-start.4
  1015.9 11.9 collective-permute-start.2
  1016.0 11.9 collective-permute-start.1
  1016.1 11.8 collective-permute-start
  1052.3 16.8 %collective-permute-start.2 = (s32[256]{0:T(256)S(1)}, s32[256]{0:T(256)S(1)}, u32[]{:S(2)}, u32[]{:S(2)}) collective-permute-start(s32[256]{0:T(256)S(1)} %copy.128), channel_id=1, source_target_pairs={{252,0},{0,4},{4,8},{8,12},{12,16},{16,20},{20,24},{24,28},{28,32}... | collective-permute-start | bytes 3080 | tf_op jit(solution)/shard_map/while/body/eval_jaxpr/ppermute | solution.py:12
  1052.3 16.8 %collective-permute-start.1 = (bf16[256,128]{1,0:T(8,128)(2,1)S(1)}, bf16[256,128]{1,0:T(8,128)(2,1)S(1)}, u32[]{:S(2)}, u32[]{:S(2)}) collective-permute-start(bf16[256,128]{1,0:T(8,128)(2,1)S(1)} %copy.127), channel_id=1, source_target_pairs={{252,0},{0,4},{4,8},{8,12},{12,16},{16,20},{20,24},{24,28},{28,32}... | collective-permute-start | bytes 196616 | tf_op jit(solution)/shard_map/while/body/eval_jaxpr/ppermute | solution.py:12
  1055.4 13.8 %collective-permute-start = (bf16[256,128]{1,0:T(8,128)(2,1)S(1)}, bf16[256,128]{1,0:T(8,128)(2,1)S(1)}, u32[]{:S(2)}, u32[]{:S(2)}) collective-permute-start(bf16[256,128]{1,0:T(8,128)(2,1)S(1)} %copy.126), channel_id=1, source_target_pairs={{252,0},{0,4},{4,8},{8,12},{12,16},{16,20},{20,24},{24,28},{28,32}... | collective-permute-start | bytes 196616 | tf_op jit(solution)/shard_map/while/body/eval_jaxpr/ppermute | solution.py:12
  1125.7 18.1 %collective-permute-start.2 = (s32[256]{0:T(256)S(1)}, s32[256]{0:T(256)S(1)}, u32[]{:S(2)}, u32[]{:S(2)}) collective-permute-start(s32[256]{0:T(256)S(1)} %copy.128), channel_id=1, source_target_pairs={{252,0},{0,4},{4,8},{8,12},{12,16},{16,20},{20,24},{24,28},{28,32}... | collective-permute-start | bytes 3080 | tf_op jit(solution)/shard_map/while/body/eval_jaxpr/ppermute | solution.py:12
  1125.7 18.1 %collective-permute-start.1 = (bf16[256,128]{1,0:T(8,128)(2,1)S(1)}, bf16[256,128]{1,0:T(8,128)(2,1)S(1)}, u32[]{:S(2)}, u32[]{:S(2)}) collective-permute-start(bf16[256,128]{1,0:T(8,128)(2,1)S(1)} %copy.127), channel_id=1, source_target_pairs={{252,0},{0,4},{4,8},{8,12},{12,16},{16,20},{20,24},{24,28},{28,32}... | collective-permute-start | bytes 196616 | tf_op jit(solution)/shard_map/while/body/eval_jaxpr/ppermute | solution.py:12
  1127.5 16.4 %collective-permute-start = (bf16[256,128]{1,0:T(8,128)(2,1)S(1)}, bf16[256,128]{1,0:T(8,128)(2,1)S(1)}, u32[]{:S(2)}, u32[]{:S(2)}) collective-permute-start(bf16[256,128]{1,0:T(8,128)(2,1)S(1)} %copy.126), channel_id=1, source_target_pairs={{252,0},{0,4},{4,8},{8,12},{12,16},{16,20},{20,24},{24,28},{28,32}... | collective-permute-start | bytes 196616 | tf_op jit(solution)/shard_map/while/body/eval_jaxpr/ppermute | solution.py:12
  1169.1 11.4 collective-permute-start.6
  (262 other events, 2458.7 us)
Sparse Core Ops, SparseCore 0:
  1179.9 175.6 all-reduce.2
where the time goes:
time: 1360 us
  waiting for transfers between devices  587 us (43%)
  starting transfers between devices  364 us (27%)
  matrix products  213 us (16%)
  blocking collectives  151 us (11%)
  other arithmetic  15.7 us (1%)
  between operations  14.3 us (1%)
    ppermute x317, waiting for transfers between devices, shifted(): return lax.ppermute(block, axis, route)  563 us
    ppermute x317, starting transfers between devices, shifted(): return lax.ppermute(block, axis, route)  364 us
    psum x1, blocking collectives, shards(): lax.psum((key_running_sum, value_running_sum), 'heads')  151 us
    dot_general x256, matrix products, tile_terms(): jnp.einsum('htk,kd->thd', dscores, key_block, preferred_element_type=jnp....  50.3 us
    dot_general x256, matrix products, tile_terms(): jnp.einsum('thd,kd->htk', qrows, key_block, preferred_element_type=jnp.fl...  45.5 us
    dot_general x256, matrix products, tile_terms(): jnp.einsum('thd,kd->htk', grows, value_block, preferred_element_type=jnp....  42.7 us
    dot_general x256, matrix products, tile_terms(): jnp.einsum('htk,thd->kd', probs.astype(jnp.bfloat16), grows, preferred_el...  37.1 us
    dot_general x256, matrix products, tile_terms(): jnp.einsum('htk,thd->kd', dscores, qrows, preferred_element_type=jnp.floa...  37 us
  transfers between devices with their start and end apart: 318, of which 229 were waited for; matrix products, arithmetic and copies ran while one was open for 17% of the time, Pallas kernels for 0%

commit v1 on v0

v1 whole, which is shorter than its diff:
```python
import functools
import math

import jax
import jax.numpy as jnp
from jax import lax
from jax.experimental import pallas as pl
from jax.experimental.pallas import tpu as pltpu
from jax.sharding import Mesh
from jax.sharding import PartitionSpec as P

HEADS = ("yl", "core")
KEY_GROUP = ("z", "x")
SWAP = [(0, 1), (1, 0)]
STEPS = [
    ("yl", SWAP),
    ("yh", SWAP),
    (("yh", "yl"), [(0, 3), (1, 2), (2, 1), (3, 0)]),
]
HALF = 128
DH = 128
PART = HALF // 4
SHARDS = 32
BLOCKS = 2 * SHARDS
KEYS = BLOCKS * PART
QROWS = 4 * HALF * 2 + 32
KROWS = 4 * PART + 8
SPAN = 8
CHUNK = SPAN * PART
VMEM_BYTES = 60 << 20
LOG2E = math.log2(math.e)
SCALE = 1.0 / math.sqrt(DH)
NT = (((1,), (1,)), ((), ()))
NN = (((1,), (0,)), ((), ()))


def dot(a, b, dims):
    return lax.dot_general(a, b, dims, preferred_element_type=jnp.float32)


def pack_kernel(block_pos, *refs):
    sources, (qmsg, kmsg), (query, key, value, output, grad, lse), sems = (
        refs[:6],
        refs[6:8],
        refs[8:14],
        refs[14],
    )
    copies = [
        pltpu.make_async_copy(src, dst, sems.at[i])
        for i, (src, dst) in enumerate(zip(sources, (query, key, value, output, grad, lse)))
    ]
    for copy in copies:
        copy.start()
    for copy in copies:
        copy.wait()
    rows = []
    drows = []
    for hb in range(2):
        for h in range(2):
            part = (slice(hb * HALF, (hb + 1) * HALF), slice(h * DH, (h + 1) * DH))
            place = (hb * 2 + h) * HALF
            qmsg[place : place + HALF, :] = query[part]
            qmsg[4 * HALF + place : 4 * HALF + place + HALF, :] = grad[part]
            prod = output[part].astype(jnp.float32) * grad[part].astype(jnp.float32)
            drows.append(jnp.sum(prod.T, axis=0, keepdims=True))
            rows.append(lse[h : h + 1, hb * HALF : (hb + 1) * HALF] * LOG2E)
    exact = jnp.concatenate(rows + drows, axis=0)
    high = exact.astype(jnp.bfloat16)
    rest = exact - high.astype(jnp.float32)
    mid = rest.astype(jnp.bfloat16)
    low = (rest - mid.astype(jnp.float32)).astype(jnp.bfloat16)
    lane = lax.broadcasted_iota(jnp.int32, (8, 128), 1)
    places = jnp.where(lane == 0, block_pos[0], block_pos[1]).astype(jnp.float32)
    extra = [v.astype(jnp.float32) for v in (high, mid, low)] + [places]
    qmsg[8 * HALF :, :] = jnp.concatenate(extra, axis=0).astype(jnp.bfloat16)

    quarter = lax.axis_index(HEADS)
    block = []
    for array in (key, value):
        for hb in range(2):
            start = pl.multiple_of(hb * HALF + quarter * PART, PART)
            block.append(array[pl.ds(start, PART), :])
    message = jnp.concatenate(block, axis=0)
    for d in range(SHARDS):
        kmsg[d, : 4 * PART, :] = message
        kmsg[d, 4 * PART :, :] = places.astype(jnp.bfloat16)


def tile_kernel(info, *refs):
    sources = refs[:9]
    dqmine, dqother, dkv = refs[9:12]
    (qs_all, kall, table, order, spos, cum, ks, vs, kst, dks, dvs, lrow, drow, dqt) = refs[12:26]
    sems = refs[26]
    places = [qs_all.at[d] for d in (0, 2, 4, 6, 1, 3, 5, 7)] + [kall]
    copies = [
        pltpu.make_async_copy(src, dst, sems.at[i])
        for i, (src, dst) in enumerate(zip(sources, places))
    ]
    for copy in reversed(copies):
        copy.start()
    quarter = lax.axis_index(HEADS)

    def clear(i, _):
        table[i] = -1
        return 0

    lax.fori_loop(0, 2 * BLOCKS, clear, 0, unroll=8)

    def enter(i, _):
        table[info[i]] = i
        return 0

    lax.fori_loop(0, BLOCKS, enter, 0, unroll=8)

    def scan(p, count):
        i = table[p]
        order[count] = i
        spos[count] = p
        count = count + jnp.where(i >= 0, 1, 0)
        cum[p] = count
        return count

    lax.fori_loop(0, 2 * BLOCKS, scan, 0, unroll=8)
    dks[...] = jnp.zeros_like(dks)
    dvs[...] = jnp.zeros_like(dvs)
    copies[8].wait()

    def place(r, _):
        i = order[r]
        src = pl.multiple_of((i % 2) * PART, PART)
        dst = pl.multiple_of(r * PART, PART)
        ks[pl.ds(dst, PART), :] = kall[i // 2, pl.ds(src, PART), :]
        vs[pl.ds(dst, PART), :] = kall[i // 2, pl.ds(src + 2 * PART, PART), :]
        return 0

    lax.fori_loop(0, BLOCKS, place, 0, unroll=8)
    for j in range(KEYS // CHUNK):
        span = slice(j * CHUNK, (j + 1) * CHUNK)
        kst[:, span] = ks[span, :].T
    for copy in copies[:8]:
        copy.wait()

    for d in range(8):
        extra = qs_all[d, 8 * HALF :, :].astype(jnp.float32)
        exact = extra[0:8] + extra[8:16] + extra[16:24]
        for hb in range(2):
            lrow[d, hb] = jnp.concatenate([exact[2 * hb : 2 * hb + 1], exact[2 * hb + 1 : 2 * hb + 2]], axis=1)
            drow[d, hb] = jnp.concatenate([exact[4 + 2 * hb : 5 + 2 * hb], exact[5 + 2 * hb : 6 + 2 * hb]], axis=1)

    gap = (
        lax.broadcasted_iota(jnp.int32, (PART, 2 * HALF), 0)
        + quarter * PART
        - lax.broadcasted_iota(jnp.int32, (PART, 2 * HALF), 1) % HALF
    )

    for hb4 in range(4):
        yh, hb = hb4 // 2, hb4 % 2
        qp = info[BLOCKS + hb4]
        seen = cum[qp]
        full = (seen - jnp.where(table[qp] >= 0, 1, 0)) // SPAN
        dqt[...] = jnp.zeros_like(dqt)

        def step(j, masked, yh=yh, hb=hb, qp=qp):
            span = pl.ds(pl.multiple_of(j * CHUNK, CHUNK), CHUNK)
            kc = ks[span, :]
            vc = vs[span, :]
            kct = kst[:, span]
            if masked:
                allowed = jnp.concatenate(
                    [gap <= (qp - spos[j * SPAN + i]) * HALF for i in range(SPAN)], axis=0
                )
            qs = [qs_all[yh * 4 + h, hb * 2 * HALF : (hb + 1) * 2 * HALF, :] for h in range(4)]
            gs = [qs_all[yh * 4 + h, (hb + 2) * 2 * HALF : (hb + 3) * 2 * HALF, :] for h in range(4)]
            low = []
            dlow = []
            for h in range(4):
                d = yh * 4 + h
                scores = dot(kc, qs[h], NT)
                probs = jnp.exp2(scores * (SCALE * LOG2E) - lrow[d, hb])
                if masked:
                    probs = jnp.where(allowed, probs, 0.0)
                dprobs = dot(vc, gs[h], NT)
                low.append(probs.astype(jnp.bfloat16))
                dlow.append((probs * (dprobs - drow[d, hb])).astype(jnp.bfloat16))
            low = jnp.concatenate(low, axis=1)
            dlow = jnp.concatenate(dlow, axis=1)
            dvs[span, :] += dot(low, jnp.concatenate(gs, axis=0), NN)
            dks[span, :] += dot(dlow, jnp.concatenate(qs, axis=0), NN)
            dqt[...] += dot(kct, dlow, NN)

        lax.fori_loop(0, full, lambda j, _, step=step: (step(j, False), 0)[1], 0)

        @pl.when(seen > full * SPAN)
        def _(step=step, full=full):
            step(full, True)

        for h in range(4):
            if h % 2 == 0:
                dqmine[yh * 2 + h // 2, hb] = dqt[:, h * 2 * HALF : (h + 1) * 2 * HALF]
            else:
                dqother[yh * 2 + h // 2, hb] = dqt[:, h * 2 * HALF : (h + 1) * 2 * HALF].astype(jnp.bfloat16)

    def restore(r, _):
        i = order[r]
        dst = pl.multiple_of((i % 2) * PART, PART)
        src = pl.multiple_of(r * PART, PART)
        dkv[i // 2, pl.ds(dst, PART), :] = dks[pl.ds(src, PART), :].astype(jnp.bfloat16)
        dkv[i // 2, pl.ds(dst + 2 * PART, PART), :] = dvs[pl.ds(src, PART), :].astype(jnp.bfloat16)
        return 0

    lax.fori_loop(0, BLOCKS, restore, 0, unroll=8)


VMEM = pl.BlockSpec(memory_space=pltpu.VMEM)
SMEM = pl.BlockSpec(memory_space=pltpu.SMEM)


def pack(block_pos, query, key, value, output, grad, lse):
    return pl.pallas_call(
        pack_kernel,
        out_shape=(
            jax.ShapeDtypeStruct((QROWS, DH), jnp.bfloat16),
            jax.ShapeDtypeStruct((SHARDS, KROWS, DH), jnp.bfloat16),
        ),
        in_specs=[SMEM] + [pl.BlockSpec(memory_space=pltpu.HBM)] * 6,
        out_specs=(VMEM, VMEM),
        scratch_shapes=[
            pltpu.VMEM(a.shape, a.dtype) for a in (query, key, value, output, grad, lse)
        ]
        + [pltpu.SemaphoreType.DMA((6,))],
        compiler_params=pltpu.CompilerParams(vmem_limit_bytes=VMEM_BYTES),
        name="pack",
    )(block_pos, query, key, value, output, grad, lse)


def tile(info, messages, kall):
    return pl.pallas_call(
        tile_kernel,
        out_shape=(
            jax.ShapeDtypeStruct((4, 2, DH, 2 * HALF), jnp.float32),
            jax.ShapeDtypeStruct((4, 2, DH, 2 * HALF), jnp.bfloat16),
            jax.ShapeDtypeStruct((SHARDS, 4 * PART, DH), jnp.bfloat16),
        ),
        in_specs=[SMEM] + [pl.BlockSpec(memory_space=pltpu.HBM)] * 9,
        out_specs=(VMEM, VMEM, VMEM),
        scratch_shapes=[
            pltpu.VMEM((8, QROWS, DH), jnp.bfloat16),
            pltpu.VMEM((SHARDS, KROWS, DH), jnp.bfloat16),
            pltpu.SMEM((2 * BLOCKS,), jnp.int32),
            pltpu.SMEM((2 * BLOCKS,), jnp.int32),
            pltpu.SMEM((2 * BLOCKS,), jnp.int32),
            pltpu.SMEM((2 * BLOCKS,), jnp.int32),
            pltpu.VMEM((KEYS, DH), jnp.bfloat16),
            pltpu.VMEM((KEYS, DH), jnp.bfloat16),
            pltpu.VMEM((DH, KEYS), jnp.bfloat16),
            pltpu.VMEM((KEYS, DH), jnp.float32),
            pltpu.VMEM((KEYS, DH), jnp.float32),
            pltpu.VMEM((8, 2, 1, 2 * HALF), jnp.float32),
            pltpu.VMEM((8, 2, 1, 2 * HALF), jnp.float32),
            pltpu.VMEM((DH, 8 * HALF), jnp.float32),
            pltpu.SemaphoreType.DMA((9,)),
        ],
        compiler_params=pltpu.CompilerParams(vmem_limit_bytes=VMEM_BYTES),
        cost_estimate=pl.CostEstimate(flops=6 * 10**9, bytes_accessed=6 << 20, transcendentals=5 * 10**6),
        name="tile",
    )(info, *messages, kall)


def shards(query, key_rows, head_value_rows, output, out_grad, logsumexp, block_pos):
    qmsg, kmsg = pack(block_pos, query, key_rows, head_value_rows, output, out_grad, logsumexp)
    kall = lax.all_to_all(kmsg, KEY_GROUP, 0, 0, tiled=True)
    near = [qmsg] + [lax.ppermute(qmsg, axes, route) for axes, route in STEPS]
    far = [lax.ppermute(message, "core", SWAP) for message in near]

    kpos = kall[:, 4 * PART, :2].astype(jnp.int32).reshape(BLOCKS)
    qpos = near[2][8 * HALF + 24, :2].astype(jnp.int32)
    info = jnp.concatenate([kpos, block_pos, qpos])
    dqmine, dqother, dkv = tile(info, near + far, kall)

    dq = dqmine + lax.ppermute(dqother, "core", SWAP).astype(jnp.float32)
    low = dq.astype(jnp.bfloat16)
    dq = dq[0]
    for i, (axes, route) in enumerate(STEPS):
        dq = dq + lax.ppermute(low[i + 1], axes, route).astype(jnp.float32)
    dkv = lax.all_to_all(dkv, KEY_GROUP, 0, 0, tiled=True)
    total = jnp.sum(dkv.astype(jnp.float32), axis=0)
    factor = jnp.where(jnp.arange(4 * PART) < 2 * PART, SCALE, 1.0).astype(jnp.float32)
    mine = (total * factor[:, None]).astype(jnp.bfloat16)
    quarters = lax.all_gather(mine, HEADS, tiled=False)
    quarters = quarters.reshape(4, 2, 2, PART, DH).transpose(1, 2, 0, 3, 4).reshape(2, 2 * HALF, DH)
    dq = (dq * SCALE).reshape(2, DH, 2, HALF).transpose(0, 3, 2, 1).reshape(2 * HALF, 2 * DH)
    return dq.astype(jnp.bfloat16), quarters[0], quarters[1]


def solution(mesh):
    split = Mesh(mesh.devices.reshape(8, 4, 2, 2, 2), ("z", "x", "yh", "yl", "core"))
    seq = ("z", "x", "yh")
    in_specs = (
        P(seq, HEADS),
        P(seq, None),
        P(seq, None),
        P(seq, HEADS),
        P(seq, HEADS),
        P(HEADS, seq),
        P(seq),
    )
    out_specs = (P(seq, HEADS), P(seq, None), P(seq, None))
    return jax.shard_map(shards, mesh=split, in_specs=in_specs, out_specs=out_specs, check_vma=False)
```

time: 1360 us -> 108 us (0.08)
  waiting for transfers between devices: 587 us -> 34.3 us
  starting transfers between devices: 364 us -> 35.6 us
  matrix products: 213 us -> 0 us
  blocking collectives: 151 us -> 9.21 us
  Pallas kernels: 0 us -> 22.5 us
  other arithmetic: 15.7 us -> 1.22 us
    ppermute x317 -> x11, waiting for transfers between devices: 563 us -> 13.6 us  [the longest x3 6.17 us: shards(): near = [qmsg] + [lax.ppermute(qmsg, axes, route) for axes, route in STEPS]]
    ppermute x317 -> x11, starting transfers between devices: 364 us -> 16.9 us  [the longest x4 6.81 us: shards(): far = [lax.ppermute(message, 'core', SWAP) for message in near]]
    dot_general x1280 -> x0, matrix products: 213 us -> none  [the longest x256 50.3 us: tile_terms(): jnp.einsum('htk,kd->thd', dscores, key_block, preferred_element_type=jnp....]
    psum x1 -> x0, blocking collectives: 151 us -> none  [shards(): lax.psum((key_running_sum, value_running_sum), 'heads')]
    psum x1 -> x0, waiting for transfers between devices: 23.9 us -> none  [shards(): lax.psum((key_running_sum, value_running_sum), 'heads')]
    pallas_call x0 -> x2, Pallas kernels: none -> 22.5 us  [the longest x1 19.4 us: tile(): pl.pallas_call(tile_kernel, out_shape=(jax.ShapeDtypeStruct((4, 2, DH, 2...]
    all_to_all x0 -> x2, waiting for transfers between devices: none -> 20.7 us  [the longest x1 10.6 us: shards(): kall = lax.all_to_all(kmsg, KEY_GROUP, 0, 0, tiled=True)]
    all_to_all x0 -> x2, starting transfers between devices: none -> 18.6 us  [the longest x1 12 us: shards(): kall = lax.all_to_all(kmsg, KEY_GROUP, 0, 0, tiled=True)]
  transfers between devices with their start and end apart: 318 -> 13, of which waited for: 229 -> 8; matrix products, arithmetic and copies ran while one was open for 17% -> 2% of each run, Pallas kernels for 0% -> 0%
where the time goes in v1:
time: 108 us; the launch traced here: 107 us
  starting transfers between devices  35.6 us (33%)
  waiting for transfers between devices  34.3 us (32%)
  Pallas kernels  22.5 us (21%)
  blocking collectives  9.21 us (9%)
  local copies, waits for them, and re-layouts  3.82 us (4%)
  other arithmetic  1.22 us (1%)
    pallas_call x1, Pallas kernels, tile(): pl.pallas_call(tile_kernel, out_shape=(jax.ShapeDtypeStruct((4, 2, DH, 2...  19.4 us
    all_to_all x1, starting transfers between devices, shards(): kall = lax.all_to_all(kmsg, KEY_GROUP, 0, 0, tiled=True)  12 us
    all_to_all x1, waiting for transfers between devices, shards(): kall = lax.all_to_all(kmsg, KEY_GROUP, 0, 0, tiled=True)  10.6 us
    all_to_all x1, waiting for transfers between devices, shards(): dkv = lax.all_to_all(dkv, KEY_GROUP, 0, 0, tiled=True)  10.1 us
    all_gather x1, blocking collectives, shards(): quarters = lax.all_gather(mine, HEADS, tiled=False)  9.21 us
    ppermute x4, starting transfers between devices, shards(): far = [lax.ppermute(message, 'core', SWAP) for message in near]  6.81 us
    all_to_all x1, starting transfers between devices, shards(): dkv = lax.all_to_all(dkv, KEY_GROUP, 0, 0, tiled=True)  6.63 us
    ppermute x3, waiting for transfers between devices, shards(): near = [qmsg] + [lax.ppermute(qmsg, axes, route) for axes, route in STEPS]  6.17 us
  transfers between devices with their start and end apart: 13, of which 8 were waited for; matrix products, arithmetic and copies ran while one was open for 2% of the time, Pallas kernels for 0%

profile of v1, /device:TPU:1, one launch (start us, length us, event | category | flops | bytes accessed | tf_op | source)
XLA Modules:
  0.0 107.5 jit_solution(1967274345087601281)
XLA Ops:
  0.6 3.1 %pack.1 = (bf16[1056,128]{1,0:T(8,128)(2,1)}, bf16[32,136,128]{2,1,0:T(8,128)(2,1)}) custom-call(s32[2]{0:T(128)} %block_pos.1, bf16[256,256]{1,0:T(8,128)(2,1)} %refs_0_.1, bf16[256,128]{1,0:T(8,128)(2,1)} %refs_1_.1, bf16[256,128]{1,0:T(8,128)(2,1)} %refs_2_.1, bf16[256,256]{1,0:T(8,128)(2,1)} %refs_3_.1, bf16[256,256]{1,0:T(8,128)(2,1)} %refs_4_.1, ...), custom_call_target="tpu_custom_call" | custom-call | tf_op jit(solution)/shard_map/pack/pallas_call | solution.py:219
  3.8 0.0 copy-start.4
  3.8 0.0 copy-start.2
  3.8 12.0 %all-to-all-start = ((bf16[32,136,128]{2,1,0:T(8,128)(2,1)}), bf16[32,136,128]{2,1,0:T(8,128)(2,1)S(1)}, u32[]{:S(2)}, u32[]{:S(2)}) async-start(bf16[32,136,128]{2,1,0:T(8,128)(2,1)} %get-tuple-element.8), calls=%async_computation | async-start | bytes 2228224 | tf_op jit(solution)/shard_map/all_to_all | solution.py:271
  15.8 0.0 copy-done.4
  15.8 3.0 %collective-permute-start = (bf16[1056,128]{1,0:T(8,128)(2,1)S(1)}, bf16[1056,128]{1,0:T(8,128)(2,1)S(1)}, u32[]{:S(2)}, u32[]{:S(2)}) collective-permute-start(bf16[1056,128]{1,0:T(8,128)(2,1)S(1)} %copy-done.4), channel_id=1, source_target_pairs={{0,4},{4,0},{1,5},{5,1},{2,6},{6,2},{3,7},{7,3},{8,12},{12,8},{9,1... | collective-permute-start | bytes 811016 | tf_op jit(solution)/shard_map/ppermute | solution.py:272
  18.8 0.4 collective-permute-start.1
  19.2 0.4 collective-permute-start.2
  19.6 1.5 %collective-permute-start.3 = (bf16[1056,128]{1,0:T(8,128)(2,1)S(1)}, bf16[1056,128]{1,0:T(8,128)(2,1)S(1)}, u32[]{:S(2)}, u32[]{:S(2)}) collective-permute-start(bf16[1056,128]{1,0:T(8,128)(2,1)S(1)} %copy-done.4), channel_id=1, source_target_pairs={{0,1},{1,0},{2,3},{3,2},{4,5},{5,4},{6,7},{7,6},{8,9},{9,8},{10,11... | collective-permute-start | bytes 811016 | tf_op jit(solution)/shard_map/ppermute | solution.py:273
  21.1 3.3 %collective-permute-done.refs_2_ = bf16[1056,128]{1,0:T(8,128)(2,1)S(1)} collective-permute-done((bf16[1056,128]{1,0:T(8,128)(2,1)S(1)}, bf16[1056,128]{1,0:T(8,128)(2,1)S(1)}, u32[]{:S(2)}, u32[]{:S(2)}) %collective-permute-start) | collective-permute-done | bytes 270368 | tf_op jit(solution)/shard_map/ppermute | solution.py:272
  24.4 0.0 copy-start.5
  24.4 3.3 %collective-permute-start.5 = (bf16[1056,128]{1,0:T(8,128)(2,1)S(1)}, bf16[1056,128]{1,0:T(8,128)(2,1)S(1)}, u32[]{:S(2)}, u32[]{:S(2)}) collective-permute-start(bf16[1056,128]{1,0:T(8,128)(2,1)S(1)} %collective-permute-done.refs_2_), channel_id=1, source_target_pairs={{0,1},{1,0},{2,3},{3,2},{4,5},{5,4},{6,7},{7,6},{8,9},{9,8},{10,11... | collective-permute-start | bytes 811016 | tf_op jit(solution)/shard_map/ppermute | solution.py:273
  27.8 2.8 %collective-permute-done.1.refs_1_ = bf16[1056,128]{1,0:T(8,128)(2,1)S(1)} collective-permute-done((bf16[1056,128]{1,0:T(8,128)(2,1)S(1)}, bf16[1056,128]{1,0:T(8,128)(2,1)S(1)}, u32[]{:S(2)}, u32[]{:S(2)}) %collective-permute-start.1) | collective-permute-done | bytes 270368 | tf_op jit(solution)/shard_map/ppermute | solution.py:272
  30.6 0.0 copy-start.6
  30.6 1.9 %collective-permute-start.4 = (bf16[1056,128]{1,0:T(8,128)(2,1)S(1)}, bf16[1056,128]{1,0:T(8,128)(2,1)S(1)}, u32[]{:S(2)}, u32[]{:S(2)}) collective-permute-start(bf16[1056,128]{1,0:T(8,128)(2,1)S(1)} %collective-permute-done.1.refs_1_), channel_id=1, source_target_pairs={{0,1},{1,0},{2,3},{3,2},{4,5},{5,4},{6,7},{7,6},{8,9},{9,8},{10,11... | collective-permute-start | bytes 811016 | tf_op jit(solution)/shard_map/ppermute | solution.py:273
  32.5 0.0 collective-permute-done.2.refs_3_
  32.5 0.0 copy-start.7
  32.5 0.1 collective-permute-start.6
  32.6 10.6 %all-to-all-done.refs_8_ = bf16[32,136,128]{2,1,0:T(8,128)(2,1)S(1)} async-done(((bf16[32,136,128]{2,1,0:T(8,128)(2,1)}), bf16[32,136,128]{2,1,0:T(8,128)(2,1)S(1)}, u32[]{:S(2)}, u32[]{:S(2)}) %all-to-all-start) | async-done | bytes 1114144 | tf_op jit(solution)/shard_map/all_to_all | solution.py:271
  43.2 0.0 copy-start
  43.2 0.1 fusion.6
  43.2 0.1 reshape.59
  43.3 0.0 copy-done.2
  43.3 0.7 pad_add_fusion.info
  44.0 0.0 collective-permute-done.3.refs_4_
  44.0 0.0 copy-start.8
  44.0 0.0 collective-permute-done.5.refs_6_
  44.0 0.0 copy-start.9
  44.1 0.0 collective-permute-done.4.refs_5_
  44.1 0.0 copy-start.10
  44.1 0.0 collective-permute-done.6.refs_7_
  44.1 0.0 copy-done.5
  44.1 0.0 copy-done.6
  44.1 0.0 copy-done.7
  44.1 0.1 copy-done
  44.2 0.6 copy-done.8
  44.7 0.1 copy-done.9
  44.8 0.1 copy-done.10
  45.0 0.0 copy-start.11
  45.0 0.7 copy-done.11
  45.7 19.4 %tile.1 = (f32[4,2,128,256]{3,2,1,0:T(8,128)}, bf16[4,2,128,256]{3,2,1,0:T(8,128)(2,1)}, bf16[32,128,128]{2,1,0:T(8,128)(2,1)}) custom-call(s32[68]{0:T(128)} %pad_add_fusion.info, bf16[1056,128]{1,0:T(8,128)(2,1)} %get-tuple-element.9.refs_0_, bf16[1056,128]{1,0:T(8,128)(2,1)} %copy-done.6, bf16[1056,128]{1,0:T(8,128)(2,1)} %copy-done.5, ...), custom_call_target="tpu_custom_call" | custom-call | flops 6000000000 | bytes 6291456 | tf_op jit(solution)/shard_map/tile/pallas_call | solution.py:237
  65.0 0.0 copy-start.3
  65.0 0.0 copy-start.1
  65.1 6.6 %all-to-all-start.1 = ((bf16[32,128,128]{2,1,0:T(8,128)(2,1)}), bf16[32,128,128]{2,1,0:T(8,128)(2,1)S(1)}, u32[]{:S(2)}, u32[]{:S(2)}) async-start(bf16[32,128,128]{2,1,0:T(8,128)(2,1)} %get-tuple-element.12), calls=%async_computation.1 | async-start | bytes 2097152 | tf_op jit(solution)/shard_map/all_to_all | solution.py:285
  71.7 0.0 copy-done.3
  71.7 2.2 %collective-permute-start.7 = (bf16[4,2,128,256]{3,2,1,0:T(8,128)(2,1)S(1)}, bf16[4,2,128,256]{3,2,1,0:T(8,128)(2,1)S(1)}, u32[]{:S(2)}, u32[]{:S(2)}) collective-permute-start(bf16[4,2,128,256]{3,2,1,0:T(8,128)(2,1)S(1)} %copy-done.3), channel_id=1, source_target_pairs={{0,1},{1,0},{2,3},{3,2},{4,5},{5,4},{6,7},{7,6},{8,9},{9,8},{10,11... | collective-permute-start | bytes 1572872 | tf_op jit(solution)/shard_map/ppermute | solution.py:280
  73.9 1.5 %collective-permute-done.7 = bf16[4,2,128,256]{3,2,1,0:T(8,128)(2,1)S(1)} collective-permute-done((bf16[4,2,128,256]{3,2,1,0:T(8,128)(2,1)S(1)}, bf16[4,2,128,256]{3,2,1,0:T(8,128)(2,1)S(1)}, u32[]{:S(2)}, u32[]{:S(2)}) %collective-permute-start.7) | collective-permute-done | bytes 524320 | tf_op jit(solution)/shard_map/ppermute | solution.py:280
  75.5 0.0 copy-done.1
  75.5 0.2 fusion.8
  75.7 2.8 %collective-permute-start.10 = (bf16[2,128,256]{2,1,0:T(8,128)(2,1)S(1)}, bf16[2,128,256]{2,1,0:T(8,128)(2,1)S(1)}, u32[]{:S(2)}, u32[]{:S(2)}) collective-permute-start(bf16[2,128,256]{2,1,0:T(8,128)(2,1)S(1)} %get-tuple-element.16), channel_id=1, source_target_pairs={{0,6},{2,4},{4,2},{6,0},{1,7},{3,5},{5,3},{7,1},{8,14},{10,12},{12... | collective-permute-start | bytes 393224 | tf_op jit(solution)/shard_map/ppermute | solution.py:284
  78.5 0.0 collective-permute-start.8
  78.5 1.3 %collective-permute-start.9 = (bf16[2,128,256]{2,1,0:T(8,128)(2,1)S(1)}, bf16[2,128,256]{2,1,0:T(8,128)(2,1)S(1)}, u32[]{:S(2)}, u32[]{:S(2)}) collective-permute-start(bf16[2,128,256]{2,1,0:T(8,128)(2,1)S(1)} %get-tuple-element.17), channel_id=1, source_target_pairs={{0,4},{4,0},{1,5},{5,1},{2,6},{6,2},{3,7},{7,3},{8,12},{12,8},{9,1... | collective-permute-start | bytes 393224 | tf_op jit(solution)/shard_map/ppermute | solution.py:284
  79.8 2.0 %collective-permute-done.10 = bf16[2,128,256]{2,1,0:T(8,128)(2,1)S(1)} collective-permute-done((bf16[2,128,256]{2,1,0:T(8,128)(2,1)S(1)}, bf16[2,128,256]{2,1,0:T(8,128)(2,1)S(1)}, u32[]{:S(2)}, u32[]{:S(2)}) %collective-permute-start.10) | collective-permute-done | bytes 131104 | tf_op jit(solution)/shard_map/ppermute | solution.py:284
  81.8 1.1 collective-permute-done.8
  82.9 2.8 %collective-permute-done.9 = bf16[2,128,256]{2,1,0:T(8,128)(2,1)S(1)} collective-permute-done((bf16[2,128,256]{2,1,0:T(8,128)(2,1)S(1)}, bf16[2,128,256]{2,1,0:T(8,128)(2,1)S(1)}, u32[]{:S(2)}, u32[]{:S(2)}) %collective-permute-start.9) | collective-permute-done | bytes 131104 | tf_op jit(solution)/shard_map/ppermute | solution.py:284
  85.7 0.1 fusion.4
  85.8 0.1 copy.15
  85.9 0.7 copy.20
  86.6 10.1 %all-to-all-done.1 = bf16[32,128,128]{2,1,0:T(8,128)(2,1)S(1)} async-done(((bf16[32,128,128]{2,1,0:T(8,128)(2,1)}), bf16[32,128,128]{2,1,0:T(8,128)(2,1)S(1)}, u32[]{:S(2)}, u32[]{:S(2)}) %all-to-all-start.1) | async-done | bytes 1048608 | tf_op jit(solution)/shard_map/all_to_all | solution.py:285
  96.7 0.2 convert_reduce_fusion
  96.9 0.1 fusion.5
  97.0 9.2 %all_gather.4 = bf16[4,128,128]{2,1,0:T(8,128)(2,1)S(1)} all-gather(bf16[1,128,128]{2,1,0:T(8,128)(2,1)S(1)} %fusion.5), channel_id=1, replica_groups=mesh['z'=8,'x'=4,'yh'=2,'yl'=2,'core'=2] {'yl','core'}, dimensions={0}, use_global_device_ids=true | all-gather | bytes 163840 | tf_op jit(solution)/shard_map/all_gather | solution.py:289
  106.2 0.6 copy.17
  106.8 0.6 copy.16
  (5 shorter events, 0.1 us)
Async XLA Ops:
  3.8 12.0 %copy-start.4 = (bf16[1056,128]{1,0:T(8,128)(2,1)S(1)}, bf16[1056,128]{1,0:T(8,128)(2,1)}, u32[]{:S(2)}) copy-start(bf16[1056,128]{1,0:T(8,128)(2,1)} %get-tuple-element.9.refs_0_) | copy-start | bytes 811012
  3.8 39.6 %copy-start.2 = (s32[2]{0:T(128)S(1)}, s32[2]{0:T(128)}, u32[]{:S(2)}) copy-start(s32[2]{0:T(128)} %block_pos.1) | copy-start | bytes 28
  3.8 39.4 %all-to-all-start = ((bf16[32,136,128]{2,1,0:T(8,128)(2,1)}), bf16[32,136,128]{2,1,0:T(8,128)(2,1)S(1)}, u32[]{:S(2)}, u32[]{:S(2)}) async-start(bf16[32,136,128]{2,1,0:T(8,128)(2,1)} %get-tuple-element.8), calls=%async_computation | async-start | bytes 2228224 | tf_op jit(solution)/shard_map/all_to_all | solution.py:271
  15.8 8.6 %collective-permute-start = (bf16[1056,128]{1,0:T(8,128)(2,1)S(1)}, bf16[1056,128]{1,0:T(8,128)(2,1)S(1)}, u32[]{:S(2)}, u32[]{:S(2)}) collective-permute-start(bf16[1056,128]{1,0:T(8,128)(2,1)S(1)} %copy-done.4), channel_id=1, source_target_pairs={{0,4},{4,0},{1,5},{5,1},{2,6},{6,2},{3,7},{7,3},{8,12},{12,8},{9,1... | collective-permute-start | bytes 811016 | tf_op jit(solution)/shard_map/ppermute | solution.py:272
  18.8 11.8 %collective-permute-start.1 = (bf16[1056,128]{1,0:T(8,128)(2,1)S(1)}, bf16[1056,128]{1,0:T(8,128)(2,1)S(1)}, u32[]{:S(2)}, u32[]{:S(2)}) collective-permute-start(bf16[1056,128]{1,0:T(8,128)(2,1)S(1)} %copy-done.4), channel_id=1, source_target_pairs={{0,2},{2,0},{1,3},{3,1},{4,6},{6,4},{5,7},{7,5},{8,10},{10,8},{9,1... | collective-permute-start | bytes 811016 | tf_op jit(solution)/shard_map/ppermute | solution.py:272
  19.2 13.3 %collective-permute-start.2 = (bf16[1056,128]{1,0:T(8,128)(2,1)S(1)}, bf16[1056,128]{1,0:T(8,128)(2,1)S(1)}, u32[]{:S(2)}, u32[]{:S(2)}) collective-permute-start(bf16[1056,128]{1,0:T(8,128)(2,1)S(1)} %copy-done.4), channel_id=1, source_target_pairs={{0,6},{2,4},{4,2},{6,0},{1,7},{3,5},{5,3},{7,1},{8,14},{10,12},{12... | collective-permute-start | bytes 811016 | tf_op jit(solution)/shard_map/ppermute | solution.py:272
  19.6 24.4 %collective-permute-start.3 = (bf16[1056,128]{1,0:T(8,128)(2,1)S(1)}, bf16[1056,128]{1,0:T(8,128)(2,1)S(1)}, u32[]{:S(2)}, u32[]{:S(2)}) collective-permute-start(bf16[1056,128]{1,0:T(8,128)(2,1)S(1)} %copy-done.4), channel_id=1, source_target_pairs={{0,1},{1,0},{2,3},{3,2},{4,5},{5,4},{6,7},{7,6},{8,9},{9,8},{10,11... | collective-permute-start | bytes 811016 | tf_op jit(solution)/shard_map/ppermute | solution.py:273
  24.4 19.7 %copy-start.5 = (bf16[1056,128]{1,0:T(8,128)(2,1)}, bf16[1056,128]{1,0:T(8,128)(2,1)S(1)}, u32[]{:S(2)}) copy-start(bf16[1056,128]{1,0:T(8,128)(2,1)S(1)} %collective-permute-done.refs_2_) | copy-start | bytes 811012
  24.4 19.6 %collective-permute-start.5 = (bf16[1056,128]{1,0:T(8,128)(2,1)S(1)}, bf16[1056,128]{1,0:T(8,128)(2,1)S(1)}, u32[]{:S(2)}, u32[]{:S(2)}) collective-permute-start(bf16[1056,128]{1,0:T(8,128)(2,1)S(1)} %collective-permute-done.refs_2_), channel_id=1, source_target_pairs={{0,1},{1,0},{2,3},{3,2},{4,5},{5,4},{6,7},{7,6},{8,9},{9,8},{10,11... | collective-permute-start | bytes 811016 | tf_op jit(solution)/shard_map/ppermute | solution.py:273
  30.6 13.5 %copy-start.6 = (bf16[1056,128]{1,0:T(8,128)(2,1)}, bf16[1056,128]{1,0:T(8,128)(2,1)S(1)}, u32[]{:S(2)}) copy-start(bf16[1056,128]{1,0:T(8,128)(2,1)S(1)} %collective-permute-done.1.refs_1_) | copy-start | bytes 811012
  30.6 13.4 %collective-permute-start.4 = (bf16[1056,128]{1,0:T(8,128)(2,1)S(1)}, bf16[1056,128]{1,0:T(8,128)(2,1)S(1)}, u32[]{:S(2)}, u32[]{:S(2)}) collective-permute-start(bf16[1056,128]{1,0:T(8,128)(2,1)S(1)} %collective-permute-done.1.refs_1_), channel_id=1, source_target_pairs={{0,1},{1,0},{2,3},{3,2},{4,5},{5,4},{6,7},{7,6},{8,9},{9,8},{10,11... | collective-permute-start | bytes 811016 | tf_op jit(solution)/shard_map/ppermute | solution.py:273
  32.5 11.6 %copy-start.7 = (bf16[1056,128]{1,0:T(8,128)(2,1)}, bf16[1056,128]{1,0:T(8,128)(2,1)S(1)}, u32[]{:S(2)}) copy-start(bf16[1056,128]{1,0:T(8,128)(2,1)S(1)} %collective-permute-done.2.refs_3_) | copy-start | bytes 811012
  32.5 11.6 %collective-permute-start.6 = (bf16[1056,128]{1,0:T(8,128)(2,1)S(1)}, bf16[1056,128]{1,0:T(8,128)(2,1)S(1)}, u32[]{:S(2)}, u32[]{:S(2)}) collective-permute-start(bf16[1056,128]{1,0:T(8,128)(2,1)S(1)} %collective-permute-done.2.refs_3_), channel_id=1, source_target_pairs={{0,1},{1,0},{2,3},{3,2},{4,5},{5,4},{6,7},{7,6},{8,9},{9,8},{10,11... | collective-permute-start | bytes 811016 | tf_op jit(solution)/shard_map/ppermute | solution.py:273
  43.2 1.0 copy-start
  44.0 0.7 copy-start.8
  44.0 0.8 copy-start.9
  44.1 0.9 copy-start.10
  45.0 0.7 copy-start.11
  65.0 6.7 %copy-start.3 = (bf16[4,2,128,256]{3,2,1,0:T(8,128)(2,1)S(1)}, bf16[4,2,128,256]{3,2,1,0:T(8,128)(2,1)}, u32[]{:S(2)}) copy-start(bf16[4,2,128,256]{3,2,1,0:T(8,128)(2,1)} %get-tuple-element.11) | copy-start | bytes 1572868
  65.0 10.4 %copy-start.1 = (f32[4,2,128,256]{3,2,1,0:T(8,128)S(1)}, f32[4,2,128,256]{3,2,1,0:T(8,128)}, u32[]{:S(2)}) copy-start(f32[4,2,128,256]{3,2,1,0:T(8,128)} %get-tuple-element.10) | copy-start | bytes 3145732
  65.1 31.7 %all-to-all-start.1 = ((bf16[32,128,128]{2,1,0:T(8,128)(2,1)}), bf16[32,128,128]{2,1,0:T(8,128)(2,1)S(1)}, u32[]{:S(2)}, u32[]{:S(2)}) async-start(bf16[32,128,128]{2,1,0:T(8,128)(2,1)} %get-tuple-element.12), calls=%async_computation.1 | async-start | bytes 2097152 | tf_op jit(solution)/shard_map/all_to_all | solution.py:285
  71.7 3.8 %collective-permute-start.7 = (bf16[4,2,128,256]{3,2,1,0:T(8,128)(2,1)S(1)}, bf16[4,2,128,256]{3,2,1,0:T(8,128)(2,1)S(1)}, u32[]{:S(2)}, u32[]{:S(2)}) collective-permute-start(bf16[4,2,128,256]{3,2,1,0:T(8,128)(2,1)S(1)} %copy-done.3), channel_id=1, source_target_pairs={{0,1},{1,0},{2,3},{3,2},{4,5},{5,4},{6,7},{7,6},{8,9},{9,8},{10,11... | collective-permute-start | bytes 1572872 | tf_op jit(solution)/shard_map/ppermute | solution.py:280
  75.7 6.1 %collective-permute-start.10 = (bf16[2,128,256]{2,1,0:T(8,128)(2,1)S(1)}, bf16[2,128,256]{2,1,0:T(8,128)(2,1)S(1)}, u32[]{:S(2)}, u32[]{:S(2)}) collective-permute-start(bf16[2,128,256]{2,1,0:T(8,128)(2,1)S(1)} %get-tuple-element.16), channel_id=1, source_target_pairs={{0,6},{2,4},{4,2},{6,0},{1,7},{3,5},{5,3},{7,1},{8,14},{10,12},{12... | collective-permute-start | bytes 393224 | tf_op jit(solution)/shard_map/ppermute | solution.py:284
  78.5 4.4 %collective-permute-start.8 = (bf16[2,128,256]{2,1,0:T(8,128)(2,1)S(1)}, bf16[2,128,256]{2,1,0:T(8,128)(2,1)S(1)}, u32[]{:S(2)}, u32[]{:S(2)}) collective-permute-start(bf16[2,128,256]{2,1,0:T(8,128)(2,1)S(1)} %get-tuple-element.15), channel_id=1, source_target_pairs={{0,2},{2,0},{1,3},{3,1},{4,6},{6,4},{5,7},{7,5},{8,10},{10,8},{9,1... | collective-permute-start | bytes 393224 | tf_op jit(solution)/shard_map/ppermute | solution.py:284
  78.5 7.2 %collective-permute-start.9 = (bf16[2,128,256]{2,1,0:T(8,128)(2,1)S(1)}, bf16[2,128,256]{2,1,0:T(8,128)(2,1)S(1)}, u32[]{:S(2)}, u32[]{:S(2)}) collective-permute-start(bf16[2,128,256]{2,1,0:T(8,128)(2,1)S(1)} %get-tuple-element.17), channel_id=1, source_target_pairs={{0,4},{4,0},{1,5},{5,1},{2,6},{6,2},{3,7},{7,3},{8,12},{12,8},{9,1... | collective-permute-start | bytes 393224 | tf_op jit(solution)/shard_map/ppermute | solution.py:284

commit v2 on v1

v2 whole, which is shorter than its diff:
```python
import functools
import math

import jax
import jax.numpy as jnp
from jax import lax
from jax.experimental import pallas as pl
from jax.experimental.pallas import tpu as pltpu
from jax.sharding import Mesh
from jax.sharding import PartitionSpec as P

HEADS = ("yl", "core")
KEY_GROUP = ("z", "x")
SWAP = [(0, 1), (1, 0)]
STEPS = [
    ("yl", SWAP),
    ("yh", SWAP),
    (("yh", "yl"), [(0, 3), (1, 2), (2, 1), (3, 0)]),
]
HALF = 128
DH = 128
PART = HALF // 4
SHARDS = 32
BLOCKS = 2 * SHARDS
KEYS = BLOCKS * PART
QROWS = 4 * HALF * 2 + 32
KROWS = 4 * PART + 16
SPAN = 8
CHUNK = SPAN * PART
VMEM_BYTES = 60 << 20
LOG2E = math.log2(math.e)
SCALE = 1.0 / math.sqrt(DH)
NT = (((1,), (1,)), ((), ()))
NN = (((1,), (0,)), ((), ()))


def dot(a, b, dims):
    return lax.dot_general(a, b, dims, preferred_element_type=jnp.float32)


def fetch(sources, places, sems):
    copies = [
        pltpu.make_async_copy(src, dst, sems.at[i])
        for i, (src, dst) in enumerate(zip(sources, places))
    ]
    for copy in copies:
        copy.start()
    return copies


def place_row(block_pos):
    lane = lax.broadcasted_iota(jnp.int32, (8, 128), 1)
    return jnp.where(lane == 0, block_pos[0], block_pos[1]).astype(jnp.float32)


def pack_keys_kernel(block_pos, key_in, value_in, kmsg, key, value, sems):
    copies = fetch((key_in, value_in), (key, value), sems)
    places = place_row(block_pos)
    places = jnp.concatenate([places, places], axis=0).astype(jnp.bfloat16)
    quarter = lax.axis_index(HEADS)
    block = []
    for array, copy in zip((key, value), copies):
        copy.wait()
        for hb in range(2):
            start = pl.multiple_of(hb * HALF + quarter * PART, PART)
            block.append(array[pl.ds(start, PART), :])
    message = jnp.concatenate(block, axis=0)
    for d in range(8):
        kmsg[d, : 4 * PART, :] = message
        kmsg[d, 4 * PART :, :] = places


def pack_queries_kernel(block_pos, *refs):
    sources, qmsg, (query, grad, output, lse), sems = refs[:4], refs[4], refs[5:9], refs[9]
    for copy in fetch(sources, (query, grad, output, lse), sems):
        copy.wait()
    rows = []
    drows = []
    for hb in range(2):
        for h in range(2):
            part = (slice(hb * HALF, (hb + 1) * HALF), slice(h * DH, (h + 1) * DH))
            place = (hb * 2 + h) * HALF
            qmsg[place : place + HALF, :] = query[part]
            qmsg[4 * HALF + place : 4 * HALF + place + HALF, :] = grad[part]
            prod = output[part].astype(jnp.float32) * grad[part].astype(jnp.float32)
            drows.append(jnp.sum(prod.T, axis=0, keepdims=True))
            rows.append(lse[h : h + 1, hb * HALF : (hb + 1) * HALF] * LOG2E)
    exact = jnp.concatenate(rows + drows, axis=0)
    high = exact.astype(jnp.bfloat16)
    rest = exact - high.astype(jnp.float32)
    mid = rest.astype(jnp.bfloat16)
    low = (rest - mid.astype(jnp.float32)).astype(jnp.bfloat16)
    extra = [v.astype(jnp.float32) for v in (high, mid, low)] + [place_row(block_pos)]
    qmsg[8 * HALF :, :] = jnp.concatenate(extra, axis=0).astype(jnp.bfloat16)


def tile_kernel(info, *refs):
    messages, columns = refs[:8], refs[8:12]
    dqmine, dqother, dkv_out = refs[12:15]
    (qall, kall, dkv, table, order, spos, cum, ks, vs, kst) = refs[15:25]
    (dks, dvs, lrow, drow, dq, half, sems, done) = refs[25:]
    key_copies = fetch(columns, [kall.at[pl.ds(8 * c, 8)] for c in range(4)], sems)
    slots = (0, 2, 4, 6, 1, 3, 5, 7)
    copies = [None] * 8
    for i in (0, 4, 1, 5, 2, 6, 3, 7):
        copies[slots[i]] = pltpu.make_async_copy(messages[i], qall.at[slots[i]], sems.at[4 + i])
        copies[slots[i]].start()
    quarter = lax.axis_index(HEADS)
    x = lax.axis_index("x")

    def clear(i, _):
        table[i] = -1
        return 0

    lax.fori_loop(0, 2 * BLOCKS, clear, 0, unroll=8)

    def enter(i, _):
        table[info[i]] = i
        return 0

    lax.fori_loop(0, BLOCKS, enter, 0, unroll=8)

    def scan(p, count):
        i = table[p]
        order[count] = i
        spos[count] = p
        count = count + jnp.where(i >= 0, 1, 0)
        cum[p] = count
        return count

    lax.fori_loop(0, 2 * BLOCKS, scan, 0, unroll=8)
    dks[...] = jnp.zeros_like(dks)
    dvs[...] = jnp.zeros_like(dvs)
    dq[...] = jnp.zeros_like(dq)
    for copy in key_copies:
        copy.wait()

    def place(r, _):
        i = order[r]
        src = pl.multiple_of((i % 2) * PART, PART)
        dst = pl.multiple_of(r * PART, PART)
        ks[pl.ds(dst, PART), :] = kall[i // 2, pl.ds(src, PART), :]
        vs[pl.ds(dst, PART), :] = kall[i // 2, pl.ds(src + 2 * PART, PART), :]
        return 0

    lax.fori_loop(0, BLOCKS, place, 0, unroll=8)
    for j in range(KEYS // CHUNK):
        span = slice(j * CHUNK, (j + 1) * CHUNK)
        kst[:, span] = ks[span, :].T

    def queries_ready(yh):
        for h in range(4):
            d = yh * 4 + h
            copies[d].wait()
            extra = qall[d, 8 * HALF :, :].astype(jnp.float32)
            exact = extra[0:8] + extra[8:16] + extra[16:24]
            for hb in range(2):
                for row, k in ((lrow, 2 * hb), (drow, 2 * hb + 4)):
                    row[hb, d] = jnp.concatenate([exact[k : k + 1], exact[k + 1 : k + 2]], axis=1)

    gap = (
        lax.broadcasted_iota(jnp.int32, (PART, 2 * HALF), 0)
        + quarter * PART
        - lax.broadcasted_iota(jnp.int32, (PART, 2 * HALF), 1) % HALF
    )

    def dq_out(hb4):
        yh, hb = hb4 // 2, hb4 % 2
        pieces = []
        for h in range(4):
            src = dq.at[hb4, :, pl.ds(h * 2 * HALF, 2 * HALF)] if h % 2 == 0 else half.at[hb4, h // 2]
            dst = (dqmine, dqother)[h % 2].at[yh * 2 + h // 2, hb]
            pieces.append(pltpu.make_async_copy(src, dst, done.at[hb4 * 4 + h]))
        return pieces

    def half_block(hb4, _):
        yh, hb = hb4 // 2, hb4 % 2
        for now in range(2):
            pl.when(hb4 == 2 * now)(functools.partial(queries_ready, now))
        qp = info[BLOCKS + hb4]
        seen = cum[qp]
        full = (seen - jnp.where(table[qp] >= 0, 1, 0)) // SPAN
        rest = seen - full * SPAN
        qrow = pl.multiple_of(hb * 2 * HALF, 2 * HALF)
        grow = pl.multiple_of((hb + 2) * 2 * HALF, 2 * HALF)

        def step(j, count, masked):
            span = pl.ds(pl.multiple_of(j * CHUNK, CHUNK), count * PART)
            kc = ks[span, :]
            vc = vs[span, :]
            if masked:
                allowed = jnp.concatenate(
                    [gap <= (qp - spos[j * SPAN + i]) * HALF for i in range(count)], axis=0
                )
            qs = [qall[yh * 4 + h, pl.ds(qrow, 2 * HALF), :] for h in range(4)]
            gs = [qall[yh * 4 + h, pl.ds(grow, 2 * HALF), :] for h in range(4)]
            low = []
            dlow = []
            for h in range(4):
                d = yh * 4 + h
                scores = dot(kc, qs[h], NT)
                probs = jnp.exp2(scores * (SCALE * LOG2E) - lrow[hb, d])
                if masked:
                    probs = jnp.where(allowed, probs, 0.0)
                dprobs = dot(vc, gs[h], NT)
                low.append(probs.astype(jnp.bfloat16))
                dlow.append((probs * (dprobs - drow[hb, d])).astype(jnp.bfloat16))
            low = jnp.concatenate(low, axis=1)
            dlow = jnp.concatenate(dlow, axis=1)
            dvs[span, :] += dot(low, jnp.concatenate(gs, axis=0), NN)
            dks[span, :] += dot(dlow, jnp.concatenate(qs, axis=0), NN)
            dq[hb4] += dot(kst[:, span], dlow, NN)

        def body(j, _):
            step(2 * j, SPAN, False)
            step(2 * j + 1, SPAN, False)
            return 0

        lax.fori_loop(0, full // 2, body, 0)

        @pl.when(full % 2 == 1)
        def _():
            step(full - 1, SPAN, False)

        @pl.when(rest > SPAN // 2)
        def _():
            step(full, SPAN, True)

        @pl.when((rest > 0) & (rest <= SPAN // 2))
        def _():
            step(full, SPAN // 2, True)

        for h in (1, 3):
            half[hb4, h // 2] = dq[hb4, :, h * 2 * HALF : (h + 1) * 2 * HALF].astype(jnp.bfloat16)
        for copy in dq_out(hb4):
            copy.start()
        return 0

    lax.fori_loop(0, 4, half_block, 0)

    def restore(r, _):
        i = order[r]
        dst = pl.multiple_of((i % 2) * PART, PART)
        src = pl.multiple_of(r * PART, PART)
        shard = i // 2 % 8 * 4 + (i // 16 + x) % 4
        dkv[shard, pl.ds(dst, PART), :] = dks[pl.ds(src, PART), :].astype(jnp.bfloat16)
        dkv[shard, pl.ds(dst + 2 * PART, PART), :] = dvs[pl.ds(src, PART), :].astype(jnp.bfloat16)
        return 0

    lax.fori_loop(0, BLOCKS, restore, 0, unroll=8)
    copy = pltpu.make_async_copy(dkv, dkv_out, sems.at[0])
    copy.start()
    for hb4 in range(4):
        for piece in dq_out(hb4):
            piece.wait()
    copy.wait()


VMEM = pl.BlockSpec(memory_space=pltpu.VMEM)
SMEM = pl.BlockSpec(memory_space=pltpu.SMEM)
HBM = pl.BlockSpec(memory_space=pltpu.HBM)


def pack(kernel, shape, block_pos, *arrays):
    return pl.pallas_call(
        kernel,
        out_shape=jax.ShapeDtypeStruct(shape, jnp.bfloat16),
        in_specs=[SMEM] + [HBM] * len(arrays),
        out_specs=VMEM,
        scratch_shapes=[pltpu.VMEM(a.shape, a.dtype) for a in arrays]
        + [pltpu.SemaphoreType.DMA((len(arrays),))],
        compiler_params=pltpu.CompilerParams(vmem_limit_bytes=VMEM_BYTES),
        name="pack",
    )(block_pos, *arrays)


def tile(info, messages, columns):
    return pl.pallas_call(
        tile_kernel,
        out_shape=(
            jax.ShapeDtypeStruct((4, 2, DH, 2 * HALF), jnp.float32),
            jax.ShapeDtypeStruct((4, 2, DH, 2 * HALF), jnp.bfloat16),
            jax.ShapeDtypeStruct((SHARDS, 4 * PART, DH), jnp.bfloat16),
        ),
        in_specs=[SMEM] + [HBM] * 12,
        out_specs=(HBM, HBM, HBM),
        scratch_shapes=[
            pltpu.VMEM((8, QROWS, DH), jnp.bfloat16),
            pltpu.VMEM((SHARDS, KROWS, DH), jnp.bfloat16),
            pltpu.VMEM((SHARDS, 4 * PART, DH), jnp.bfloat16),
            pltpu.SMEM((2 * BLOCKS,), jnp.int32),
            pltpu.SMEM((2 * BLOCKS,), jnp.int32),
            pltpu.SMEM((2 * BLOCKS,), jnp.int32),
            pltpu.SMEM((2 * BLOCKS,), jnp.int32),
            pltpu.VMEM((KEYS, DH), jnp.bfloat16),
            pltpu.VMEM((KEYS, DH), jnp.bfloat16),
            pltpu.VMEM((DH, KEYS), jnp.bfloat16),
            pltpu.VMEM((KEYS, DH), jnp.float32),
            pltpu.VMEM((KEYS, DH), jnp.float32),
            pltpu.VMEM((2, 8, 1, 2 * HALF), jnp.float32),
            pltpu.VMEM((2, 8, 1, 2 * HALF), jnp.float32),
            pltpu.VMEM((4, DH, 8 * HALF), jnp.float32),
            pltpu.VMEM((4, 2, DH, 2 * HALF), jnp.bfloat16),
            pltpu.SemaphoreType.DMA((12,)),
            pltpu.SemaphoreType.DMA((16,)),
        ],
        compiler_params=pltpu.CompilerParams(vmem_limit_bytes=VMEM_BYTES),
        cost_estimate=pl.CostEstimate(flops=6 * 10**9, bytes_accessed=6 << 20, transcendentals=5 * 10**6),
        name="tile",
    )(info, *messages, *columns)


def moved(distance, size):
    return [(i, (i + distance) % size) for i in range(size)]


def shards(query, key_rows, head_value_rows, output, out_grad, logsumexp, block_pos):
    kmsg = pack(pack_keys_kernel, (8, KROWS, DH), block_pos, key_rows, head_value_rows)
    qmsg = pack(pack_queries_kernel, (QROWS, DH), block_pos, query, out_grad, output, logsumexp)
    column = lax.all_to_all(kmsg, "z", 0, 0, tiled=True)
    column, qmsg = lax.optimization_barrier((column, qmsg))
    columns = [column] + [lax.ppermute(column, "x", moved(-d, 4)) for d in (2, 1, 3)]
    columns = [columns[0], columns[2], columns[1], columns[3]]
    near = [qmsg] + [lax.ppermute(qmsg, axes, route) for axes, route in STEPS]
    far = [lax.ppermute(message, "core", SWAP) for message in near]

    places = [c[:, 4 * PART, :2].reshape(16) for c in columns]
    here = jnp.concatenate([block_pos.astype(jnp.bfloat16), near[2][8 * HALF + 24, :2]])
    info = jnp.concatenate(places + [here]).astype(jnp.int32)
    dqmine, dqother, dkv = tile(info, near + far, columns)

    dq = dqmine + lax.ppermute(dqother, "core", SWAP).astype(jnp.float32)
    low = dq.astype(jnp.bfloat16)
    dq = dq[0]
    for i, (axes, route) in enumerate(STEPS):
        dq = dq + lax.ppermute(low[i + 1], axes, route).astype(jnp.float32)
    dkv = lax.all_to_all(dkv, KEY_GROUP, 0, 0, tiled=True)
    total = jnp.sum(dkv.astype(jnp.float32), axis=0)
    factor = jnp.where(jnp.arange(4 * PART) < 2 * PART, SCALE, 1.0).astype(jnp.float32)
    mine = (total * factor[:, None]).astype(jnp.bfloat16)
    quarters = lax.all_gather(mine, HEADS, tiled=False)
    quarters = quarters.reshape(4, 2, 2, PART, DH).transpose(1, 2, 0, 3, 4).reshape(2, 2 * HALF, DH)
    dq = (dq * SCALE).reshape(2, DH, 2, HALF).transpose(0, 3, 2, 1).reshape(2 * HALF, 2 * DH)
    return dq.astype(jnp.bfloat16), quarters[0], quarters[1]


def solution(mesh):
    split = Mesh(mesh.devices.reshape(8, 4, 2, 2, 2), ("z", "x", "yh", "yl", "core"))
    seq = ("z", "x", "yh")
    in_specs = (
        P(seq, HEADS),
        P(seq, None),
        P(seq, None),
        P(seq, HEADS),
        P(seq, HEADS),
        P(HEADS, seq),
        P(seq),
    )
    out_specs = (P(seq, HEADS), P(seq, None), P(seq, None))
    return jax.shard_map(shards, mesh=split, in_specs=in_specs, out_specs=out_specs, check_vma=False)
```

time: 108 us -> 105 us (0.972)
  starting transfers between devices: 35.6 us -> 33.2 us
    ppermute x0 -> x3, starting transfers between devices: none -> 4.21 us  [shards(): lax.ppermute(column, 'x', moved(-d, 4))]
    all_to_all x1, starting transfers between devices: 12 us -> 9.03 us  [shards(): column = lax.all_to_all(kmsg, 'z', 0, 0, tiled=True)]
    all_to_all x1, waiting for transfers between devices: 10.6 us -> 8.59 us  [shards(): column = lax.all_to_all(kmsg, 'z', 0, 0, tiled=True)]
    pallas_call x1 -> x2, Pallas kernels: 3.13 us -> 5 us  [pack(): pl.pallas_call(kernel, out_shape=jax.ShapeDtypeStruct(shape, jnp.bfloat16...]
    ppermute x4, starting transfers between devices: 6.81 us -> 5.2 us  [shards(): far = [lax.ppermute(message, 'core', SWAP) for message in near]]
    pallas_call x1, Pallas kernels: 19.4 us -> 18.1 us  [tile(): pl.pallas_call(tile_kernel, out_shape=(jax.ShapeDtypeStruct((4, 2, DH, 2...]
    all_to_all x1, starting transfers between devices: 6.63 us -> 5.41 us  [shards(): dkv = lax.all_to_all(dkv, KEY_GROUP, 0, 0, tiled=True)]
    unnamed x25 -> x29, local copies, waits for them, and re-layouts: 2.25 us -> 2.23 us
  transfers between devices with their start and end apart: 13 -> 16, of which waited for: 8 -> 10; matrix products, arithmetic and copies ran while one was open for 2% -> 2% of each run, Pallas kernels for 0% -> 2%
where the time goes in v2:
time: 105 us
  waiting for transfers between devices  34.1 us (32%)
  starting transfers between devices  33.2 us (32%)
  Pallas kernels  23.2 us (22%)
  blocking collectives  8.48 us (8%)
  local copies, waits for them, and re-layouts  4.24 us (4%)
    pallas_call x1, Pallas kernels, tile(): pl.pallas_call(tile_kernel, out_shape=(jax.ShapeDtypeStruct((4, 2, DH, 2...  18.1 us
    all_to_all x1, waiting for transfers between devices, shards(): dkv = lax.all_to_all(dkv, KEY_GROUP, 0, 0, tiled=True)  10.5 us
    all_to_all x1, starting transfers between devices, shards(): column = lax.all_to_all(kmsg, 'z', 0, 0, tiled=True)  9.03 us
    all_to_all x1, waiting for transfers between devices, shards(): column = lax.all_to_all(kmsg, 'z', 0, 0, tiled=True)  8.59 us
    all_gather x1, blocking collectives, shards(): quarters = lax.all_gather(mine, HEADS, tiled=False)  8.48 us
    ppermute x3, waiting for transfers between devices, shards(): dq = dq + lax.ppermute(low[i + 1], axes, route).astype(jnp.float32)  6.97 us
    ppermute x3, waiting for transfers between devices, shards(): near = [qmsg] + [lax.ppermute(qmsg, axes, route) for axes, route in STEPS]  6.31 us
    all_to_all x1, starting transfers between devices, shards(): dkv = lax.all_to_all(dkv, KEY_GROUP, 0, 0, tiled=True)  5.41 us
  transfers between devices with their start and end apart: 16, of which 10 were waited for; matrix products, arithmetic and copies ran while one was open for 2% of the time, Pallas kernels for 2%

profile of v2, /device:TPU:1, one launch (start us, length us, event | category | flops | bytes accessed | tf_op | source)
XLA Modules:
  0.0 104.9 jit_solution(15138890627208355310)
XLA Ops:
  0.6 0.0 copy-start.2
  0.6 2.4 %pack.2 = bf16[8,144,128]{2,1,0:T(8,128)(2,1)} custom-call(s32[2]{0:T(128)} %block_pos.3, bf16[256,128]{1,0:T(8,128)(2,1)} %key_in.1, bf16[256,128]{1,0:T(8,128)(2,1)} %value_in.1), custom_call_target="tpu_custom_call" | custom-call | tf_op jit(solution)/shard_map/pack/pallas_call | solution.py:265
  3.1 9.0 %all-to-all-start = ((bf16[8,144,128]{2,1,0:T(8,128)(2,1)}), bf16[8,144,128]{2,1,0:T(8,128)(2,1)S(1)}, u32[]{:S(2)}, u32[]{:S(2)}) async-start(bf16[8,144,128]{2,1,0:T(8,128)(2,1)} %pack.2), calls=%async_computation | async-start | bytes 589824 | tf_op jit(solution)/shard_map/all_to_all | solution.py:320
  12.1 2.6 %pack.3.refs_0_ = bf16[1056,128]{1,0:T(8,128)(2,1)} custom-call(s32[2]{0:T(128)} %block_pos.3, bf16[256,256]{1,0:T(8,128)(2,1)} %refs_0_.1, bf16[256,256]{1,0:T(8,128)(2,1)} %refs_1_.1, bf16[256,256]{1,0:T(8,128)(2,1)} %refs_2_.1, f32[2,256]{1,0:T(2,128)} %refs_3_.1), custom_call_target="tpu_custom_call" | custom-call | tf_op jit(solution)/shard_map/pack/pallas_call | solution.py:265
  14.7 8.6 %all-to-all-done.refs_8_ = bf16[8,144,128]{2,1,0:T(8,128)(2,1)S(1)} async-done(((bf16[8,144,128]{2,1,0:T(8,128)(2,1)}), bf16[8,144,128]{2,1,0:T(8,128)(2,1)S(1)}, u32[]{:S(2)}, u32[]{:S(2)}) %all-to-all-start) | async-done | bytes 294944 | tf_op jit(solution)/shard_map/all_to_all | solution.py:320
  23.3 2.9 %collective-permute-start.3 = (bf16[1056,128]{1,0:T(8,128)(2,1)}, bf16[1056,128]{1,0:T(8,128)(2,1)S(1)}, u32[]{:S(2)}, u32[]{:S(2)}) collective-permute-start(bf16[1056,128]{1,0:T(8,128)(2,1)} %pack.3.refs_0_), channel_id=1, source_target_pairs={{0,4},{4,0},{1,5},{5,1},{2,6},{6,2},{3,7},{7,3},{8,12},{12,8},{9,1... | collective-permute-start | bytes 811016 | tf_op jit(solution)/shard_map/ppermute | solution.py:324
  26.2 0.0 copy-done.2
  26.2 2.5 %collective-permute-start = (bf16[8,144,128]{2,1,0:T(8,128)(2,1)S(1)}, bf16[8,144,128]{2,1,0:T(8,128)(2,1)S(1)}, u32[]{:S(2)}, u32[]{:S(2)}) collective-permute-start(bf16[8,144,128]{2,1,0:T(8,128)(2,1)S(1)} %all-to-all-done.refs_8_), channel_id=1, source_target_pairs={{0,24},{8,0},{16,8},{24,16},{1,25},{9,1},{17,9},{25,17},{2,26},{10... | collective-permute-start | bytes 884744 | tf_op jit(solution)/shard_map/ppermute | solution.py:322
  28.7 0.5 collective-permute-start.1
  29.2 0.4 collective-permute-start.4
  29.6 0.4 collective-permute-start.5
  30.0 0.1 reshape_squeeze.12
  30.1 0.2 collective-permute-done.3.refs_2_
  30.3 1.2 %collective-permute-start.2 = (bf16[8,144,128]{2,1,0:T(8,128)(2,1)S(1)}, bf16[8,144,128]{2,1,0:T(8,128)(2,1)S(1)}, u32[]{:S(2)}, u32[]{:S(2)}) collective-permute-start(bf16[8,144,128]{2,1,0:T(8,128)(2,1)S(1)} %all-to-all-done.refs_8_), channel_id=1, source_target_pairs={{0,8},{8,16},{16,24},{24,0},{1,9},{9,17},{17,25},{25,1},{2,10},{10... | collective-permute-start | bytes 884744 | tf_op jit(solution)/shard_map/ppermute | solution.py:322
  31.5 6.1 %collective-permute-done.4.refs_1_ = bf16[1056,128]{1,0:T(8,128)(2,1)S(1)} collective-permute-done((bf16[1056,128]{1,0:T(8,128)(2,1)}, bf16[1056,128]{1,0:T(8,128)(2,1)S(1)}, u32[]{:S(2)}, u32[]{:S(2)}) %collective-permute-start.4) | collective-permute-done | bytes 270368 | tf_op jit(solution)/shard_map/ppermute | solution.py:324
  37.6 2.4 %collective-permute-start.6 = (bf16[1056,128]{1,0:T(8,128)(2,1)}, bf16[1056,128]{1,0:T(8,128)(2,1)S(1)}, u32[]{:S(2)}, u32[]{:S(2)}) collective-permute-start(bf16[1056,128]{1,0:T(8,128)(2,1)} %pack.3.refs_0_), channel_id=1, source_target_pairs={{0,1},{1,0},{2,3},{3,2},{4,5},{5,4},{6,7},{7,6},{8,9},{9,8},{10,11... | collective-permute-start | bytes 811016 | tf_op jit(solution)/shard_map/ppermute | solution.py:325
  40.0 0.0 collective-permute-done.5.refs_3_
  40.0 0.9 collective-permute-start.8
  41.0 0.0 collective-permute-done.refs_9_
  41.0 1.2 %collective-permute-start.7 = (bf16[1056,128]{1,0:T(8,128)(2,1)S(1)}, bf16[1056,128]{1,0:T(8,128)(2,1)S(1)}, u32[]{:S(2)}, u32[]{:S(2)}) collective-permute-start(bf16[1056,128]{1,0:T(8,128)(2,1)S(1)} %collective-permute-done.4.refs_1_), channel_id=1, source_target_pairs={{0,1},{1,0},{2,3},{3,2},{4,5},{5,4},{6,7},{7,6},{8,9},{9,8},{10,11... | collective-permute-start | bytes 811016 | tf_op jit(solution)/shard_map/ppermute | solution.py:325
  42.2 0.0 collective-permute-done.1.refs_10_
  42.2 0.6 collective-permute-start.9
  42.9 0.1 reshape_squeeze.13
  43.0 0.1 reshape_squeeze.14
  43.1 0.1 collective-permute-done.2.refs_11_
  43.2 0.1 reshape_squeeze.15
  43.3 0.1 concatenate.3
  43.4 0.5 convert_element_type.47.info
  43.9 0.0 collective-permute-done.6.refs_4_
  43.9 0.0 collective-permute-done.8.refs_6_
  43.9 0.0 copy-start.11
  43.9 0.0 collective-permute-done.7.refs_5_
  43.9 0.1 collective-permute-done.9.refs_7_
  44.0 0.0 copy-done.9
  44.0 0.0 copy-done.3
  44.0 0.0 copy-done.4
  44.0 0.0 copy-done.5
  44.1 0.6 copy-done.10
  44.6 0.1 copy-done.11
  44.7 0.1 copy-done.12
  44.9 0.7 copy-done.13
  45.6 18.1 %tile.1 = (f32[4,2,128,256]{3,2,1,0:T(8,128)}, bf16[4,2,128,256]{3,2,1,0:T(8,128)(2,1)}, bf16[32,128,128]{2,1,0:T(8,128)(2,1)}) custom-call(s32[68]{0:T(128)} %convert_element_type.47.info, bf16[1056,128]{1,0:T(8,128)(2,1)} %pack.3.refs_0_, bf16[1056,128]{1,0:T(8,128)(2,1)} %copy-done.8, bf16[1056,128]{1,0:T(8,128)(2,1)} %copy-done.7, ...), custom_call_target="tpu_custom_call" | custom-call | flops 6000000000 | bytes 6291456 | tf_op jit(solution)/shard_map/tile/pallas_call | solution.py:278
  63.7 0.0 copy-start.6
  63.7 0.0 copy-start
  63.7 5.4 %all-to-all-start.1 = ((bf16[32,128,128]{2,1,0:T(8,128)(2,1)}), bf16[32,128,128]{2,1,0:T(8,128)(2,1)S(1)}, u32[]{:S(2)}, u32[]{:S(2)}) async-start(bf16[32,128,128]{2,1,0:T(8,128)(2,1)} %get-tuple-element.12), calls=%async_computation.1 | async-start | bytes 2097152 | tf_op jit(solution)/shard_map/all_to_all | solution.py:337
  69.2 0.0 copy-done.6
  69.2 1.7 %collective-permute-start.10 = (bf16[4,2,128,256]{3,2,1,0:T(8,128)(2,1)S(1)}, bf16[4,2,128,256]{3,2,1,0:T(8,128)(2,1)S(1)}, u32[]{:S(2)}, u32[]{:S(2)}) collective-permute-start(bf16[4,2,128,256]{3,2,1,0:T(8,128)(2,1)S(1)} %copy-done.6), channel_id=1, source_target_pairs={{0,1},{1,0},{2,3},{3,2},{4,5},{5,4},{6,7},{7,6},{8,9},{9,8},{10,11... | collective-permute-start | bytes 1572872 | tf_op jit(solution)/shard_map/ppermute | solution.py:332
  70.9 1.5 %collective-permute-done.10 = bf16[4,2,128,256]{3,2,1,0:T(8,128)(2,1)S(1)} collective-permute-done((bf16[4,2,128,256]{3,2,1,0:T(8,128)(2,1)S(1)}, bf16[4,2,128,256]{3,2,1,0:T(8,128)(2,1)S(1)}, u32[]{:S(2)}, u32[]{:S(2)}) %collective-permute-start.10) | collective-permute-done | bytes 524320 | tf_op jit(solution)/shard_map/ppermute | solution.py:332
  72.4 0.2 fusion.6
  72.6 0.5 collective-permute-start.11
  73.1 1.9 %collective-permute-start.12 = (bf16[2,128,256]{2,1,0:T(8,128)(2,1)S(1)}, bf16[2,128,256]{2,1,0:T(8,128)(2,1)S(1)}, u32[]{:S(2)}, u32[]{:S(2)}) collective-permute-start(bf16[2,128,256]{2,1,0:T(8,128)(2,1)S(1)} %get-tuple-element.17), channel_id=1, source_target_pairs={{0,4},{4,0},{1,5},{5,1},{2,6},{6,2},{3,7},{7,3},{8,12},{12,8},{9,1... | collective-permute-start | bytes 393224 | tf_op jit(solution)/shard_map/ppermute | solution.py:336
  74.9 1.6 %collective-permute-start.13 = (bf16[2,128,256]{2,1,0:T(8,128)(2,1)S(1)}, bf16[2,128,256]{2,1,0:T(8,128)(2,1)S(1)}, u32[]{:S(2)}, u32[]{:S(2)}) collective-permute-start(bf16[2,128,256]{2,1,0:T(8,128)(2,1)S(1)} %get-tuple-element.16), channel_id=1, source_target_pairs={{0,6},{2,4},{4,2},{6,0},{1,7},{3,5},{5,3},{7,1},{8,14},{10,12},{12... | collective-permute-start | bytes 393224 | tf_op jit(solution)/shard_map/ppermute | solution.py:336
  76.6 0.8 collective-permute-done.11
  77.4 3.6 %collective-permute-done.12 = bf16[2,128,256]{2,1,0:T(8,128)(2,1)S(1)} collective-permute-done((bf16[2,128,256]{2,1,0:T(8,128)(2,1)S(1)}, bf16[2,128,256]{2,1,0:T(8,128)(2,1)S(1)}, u32[]{:S(2)}, u32[]{:S(2)}) %collective-permute-start.12) | collective-permute-done | bytes 131104 | tf_op jit(solution)/shard_map/ppermute | solution.py:336
  81.0 2.5 %collective-permute-done.13 = bf16[2,128,256]{2,1,0:T(8,128)(2,1)S(1)} collective-permute-done((bf16[2,128,256]{2,1,0:T(8,128)(2,1)S(1)}, bf16[2,128,256]{2,1,0:T(8,128)(2,1)S(1)}, u32[]{:S(2)}, u32[]{:S(2)}) %collective-permute-start.13) | collective-permute-done | bytes 131104 | tf_op jit(solution)/shard_map/ppermute | solution.py:336
  83.5 0.1 fusion.4
  83.6 0.1 copy.15
  83.8 0.7 copy.20
  84.5 10.5 %all-to-all-done.1 = bf16[32,128,128]{2,1,0:T(8,128)(2,1)S(1)} async-done(((bf16[32,128,128]{2,1,0:T(8,128)(2,1)}), bf16[32,128,128]{2,1,0:T(8,128)(2,1)S(1)}, u32[]{:S(2)}, u32[]{:S(2)}) %all-to-all-start.1) | async-done | bytes 1048608 | tf_op jit(solution)/shard_map/all_to_all | solution.py:337
  94.9 0.2 convert_reduce_fusion
  95.1 0.1 fusion.5
  95.2 8.5 %all_gather.4 = bf16[4,128,128]{2,1,0:T(8,128)(2,1)S(1)} all-gather(bf16[1,128,128]{2,1,0:T(8,128)(2,1)S(1)} %fusion.5), channel_id=1, replica_groups=mesh['z'=8,'x'=4,'yh'=2,'yl'=2,'core'=2] {'yl','core'}, dimensions={0}, use_global_device_ids=true | all-gather | bytes 163840 | tf_op jit(solution)/shard_map/all_gather | solution.py:341
  103.7 0.6 copy.17
  104.3 0.6 copy.16
  (24 shorter events, 0.2 us)
Async XLA Ops:
  0.6 25.6 %copy-start.2 = (s32[2]{0:T(128)S(1)}, s32[2]{0:T(128)}, u32[]{:S(2)}) copy-start(s32[2]{0:T(128)} %block_pos.3) | copy-start | bytes 28
  3.1 20.2 %all-to-all-start = ((bf16[8,144,128]{2,1,0:T(8,128)(2,1)}), bf16[8,144,128]{2,1,0:T(8,128)(2,1)S(1)}, u32[]{:S(2)}, u32[]{:S(2)}) async-start(bf16[8,144,128]{2,1,0:T(8,128)(2,1)} %pack.2), calls=%async_computation | async-start | bytes 589824 | tf_op jit(solution)/shard_map/all_to_all | solution.py:320
  23.3 20.7 %copy-start.1 = (bf16[8,144,128]{2,1,0:T(8,128)(2,1)}, bf16[8,144,128]{2,1,0:T(8,128)(2,1)S(1)}, u32[]{:S(2)}) copy-start(bf16[8,144,128]{2,1,0:T(8,128)(2,1)S(1)} %all-to-all-done.refs_8_) | copy-start | bytes 884740
  23.3 7.0 %collective-permute-start.3 = (bf16[1056,128]{1,0:T(8,128)(2,1)}, bf16[1056,128]{1,0:T(8,128)(2,1)S(1)}, u32[]{:S(2)}, u32[]{:S(2)}) collective-permute-start(bf16[1056,128]{1,0:T(8,128)(2,1)} %pack.3.refs_0_), channel_id=1, source_target_pairs={{0,4},{4,0},{1,5},{5,1},{2,6},{6,2},{3,7},{7,3},{8,12},{12,8},{9,1... | collective-permute-start | bytes 811016 | tf_op jit(solution)/shard_map/ppermute | solution.py:324
  26.2 14.8 %collective-permute-start = (bf16[8,144,128]{2,1,0:T(8,128)(2,1)S(1)}, bf16[8,144,128]{2,1,0:T(8,128)(2,1)S(1)}, u32[]{:S(2)}, u32[]{:S(2)}) collective-permute-start(bf16[8,144,128]{2,1,0:T(8,128)(2,1)S(1)} %all-to-all-done.refs_8_), channel_id=1, source_target_pairs={{0,24},{8,0},{16,8},{24,16},{1,25},{9,1},{17,9},{25,17},{2,26},{10... | collective-permute-start | bytes 884744 | tf_op jit(solution)/shard_map/ppermute | solution.py:322
  28.7 13.5 %collective-permute-start.1 = (bf16[8,144,128]{2,1,0:T(8,128)(2,1)S(1)}, bf16[8,144,128]{2,1,0:T(8,128)(2,1)S(1)}, u32[]{:S(2)}, u32[]{:S(2)}) collective-permute-start(bf16[8,144,128]{2,1,0:T(8,128)(2,1)S(1)} %all-to-all-done.refs_8_), channel_id=1, source_target_pairs={{0,16},{8,24},{16,0},{24,8},{1,17},{9,25},{17,1},{25,9},{2,18},{10... | collective-permute-start | bytes 884744 | tf_op jit(solution)/shard_map/ppermute | solution.py:322
  29.2 8.4 %collective-permute-start.4 = (bf16[1056,128]{1,0:T(8,128)(2,1)}, bf16[1056,128]{1,0:T(8,128)(2,1)S(1)}, u32[]{:S(2)}, u32[]{:S(2)}) collective-permute-start(bf16[1056,128]{1,0:T(8,128)(2,1)} %pack.3.refs_0_), channel_id=1, source_target_pairs={{0,2},{2,0},{1,3},{3,1},{4,6},{6,4},{5,7},{7,5},{8,10},{10,8},{9,1... | collective-permute-start | bytes 811016 | tf_op jit(solution)/shard_map/ppermute | solution.py:324
  29.6 10.4 %collective-permute-start.5 = (bf16[1056,128]{1,0:T(8,128)(2,1)}, bf16[1056,128]{1,0:T(8,128)(2,1)S(1)}, u32[]{:S(2)}, u32[]{:S(2)}) collective-permute-start(bf16[1056,128]{1,0:T(8,128)(2,1)} %pack.3.refs_0_), channel_id=1, source_target_pairs={{0,6},{2,4},{4,2},{6,0},{1,7},{3,5},{5,3},{7,1},{8,14},{10,12},{12... | collective-permute-start | bytes 811016 | tf_op jit(solution)/shard_map/ppermute | solution.py:324
  30.3 13.7 %copy-start.7 = (bf16[1056,128]{1,0:T(8,128)(2,1)}, bf16[1056,128]{1,0:T(8,128)(2,1)S(1)}, u32[]{:S(2)}) copy-start(bf16[1056,128]{1,0:T(8,128)(2,1)S(1)} %collective-permute-done.3.refs_2_) | copy-start | bytes 811012
  30.3 12.9 %collective-permute-start.2 = (bf16[8,144,128]{2,1,0:T(8,128)(2,1)S(1)}, bf16[8,144,128]{2,1,0:T(8,128)(2,1)S(1)}, u32[]{:S(2)}, u32[]{:S(2)}) collective-permute-start(bf16[8,144,128]{2,1,0:T(8,128)(2,1)S(1)} %all-to-all-done.refs_8_), channel_id=1, source_target_pairs={{0,8},{8,16},{16,24},{24,0},{1,9},{9,17},{17,25},{25,1},{2,10},{10... | collective-permute-start | bytes 884744 | tf_op jit(solution)/shard_map/ppermute | solution.py:322
  37.6 6.4 %copy-start.8 = (bf16[1056,128]{1,0:T(8,128)(2,1)}, bf16[1056,128]{1,0:T(8,128)(2,1)S(1)}, u32[]{:S(2)}) copy-start(bf16[1056,128]{1,0:T(8,128)(2,1)S(1)} %collective-permute-done.4.refs_1_) | copy-start | bytes 811012
  37.6 6.3 %collective-permute-start.6 = (bf16[1056,128]{1,0:T(8,128)(2,1)}, bf16[1056,128]{1,0:T(8,128)(2,1)S(1)}, u32[]{:S(2)}, u32[]{:S(2)}) collective-permute-start(bf16[1056,128]{1,0:T(8,128)(2,1)} %pack.3.refs_0_), channel_id=1, source_target_pairs={{0,1},{1,0},{2,3},{3,2},{4,5},{5,4},{6,7},{7,6},{8,9},{9,8},{10,11... | collective-permute-start | bytes 811016 | tf_op jit(solution)/shard_map/ppermute | solution.py:325
  40.0 4.0 %copy-start.9 = (bf16[1056,128]{1,0:T(8,128)(2,1)}, bf16[1056,128]{1,0:T(8,128)(2,1)S(1)}, u32[]{:S(2)}) copy-start(bf16[1056,128]{1,0:T(8,128)(2,1)S(1)} %collective-permute-done.5.refs_3_) | copy-start | bytes 811012
  40.0 3.9 %collective-permute-start.8 = (bf16[1056,128]{1,0:T(8,128)(2,1)S(1)}, bf16[1056,128]{1,0:T(8,128)(2,1)S(1)}, u32[]{:S(2)}, u32[]{:S(2)}) collective-permute-start(bf16[1056,128]{1,0:T(8,128)(2,1)S(1)} %collective-permute-done.3.refs_2_), channel_id=1, source_target_pairs={{0,1},{1,0},{2,3},{3,2},{4,5},{5,4},{6,7},{7,6},{8,9},{9,8},{10,11... | collective-permute-start | bytes 811016 | tf_op jit(solution)/shard_map/ppermute | solution.py:325
  41.0 3.1 %copy-start.3 = (bf16[8,144,128]{2,1,0:T(8,128)(2,1)}, bf16[8,144,128]{2,1,0:T(8,128)(2,1)S(1)}, u32[]{:S(2)}) copy-start(bf16[8,144,128]{2,1,0:T(8,128)(2,1)S(1)} %collective-permute-done.refs_9_) | copy-start | bytes 884740
  41.0 2.9 %collective-permute-start.7 = (bf16[1056,128]{1,0:T(8,128)(2,1)S(1)}, bf16[1056,128]{1,0:T(8,128)(2,1)S(1)}, u32[]{:S(2)}, u32[]{:S(2)}) collective-permute-start(bf16[1056,128]{1,0:T(8,128)(2,1)S(1)} %collective-permute-done.4.refs_1_), channel_id=1, source_target_pairs={{0,1},{1,0},{2,3},{3,2},{4,5},{5,4},{6,7},{7,6},{8,9},{9,8},{10,11... | collective-permute-start | bytes 811016 | tf_op jit(solution)/shard_map/ppermute | solution.py:325
  42.2 1.8 %copy-start.4 = (bf16[8,144,128]{2,1,0:T(8,128)(2,1)}, bf16[8,144,128]{2,1,0:T(8,128)(2,1)S(1)}, u32[]{:S(2)}) copy-start(bf16[8,144,128]{2,1,0:T(8,128)(2,1)S(1)} %collective-permute-done.1.refs_10_) | copy-start | bytes 884740
  42.2 1.8 %collective-permute-start.9 = (bf16[1056,128]{1,0:T(8,128)(2,1)S(1)}, bf16[1056,128]{1,0:T(8,128)(2,1)S(1)}, u32[]{:S(2)}, u32[]{:S(2)}) collective-permute-start(bf16[1056,128]{1,0:T(8,128)(2,1)S(1)} %collective-permute-done.5.refs_3_), channel_id=1, source_target_pairs={{0,1},{1,0},{2,3},{3,2},{4,5},{5,4},{6,7},{7,6},{8,9},{9,8},{10,11... | collective-permute-start | bytes 811016 | tf_op jit(solution)/shard_map/ppermute | solution.py:325
  43.2 0.9 copy-start.5
  43.9 0.7 copy-start.10
  43.9 0.8 copy-start.11
  43.9 0.9 copy-start.12
  44.9 0.7 copy-start.13
  63.7 5.4 %copy-start.6 = (bf16[4,2,128,256]{3,2,1,0:T(8,128)(2,1)S(1)}, bf16[4,2,128,256]{3,2,1,0:T(8,128)(2,1)}, u32[]{:S(2)}) copy-start(bf16[4,2,128,256]{3,2,1,0:T(8,128)(2,1)} %get-tuple-element.11) | copy-start | bytes 1572868
  63.7 8.7 %copy-start = (f32[4,2,128,256]{3,2,1,0:T(8,128)S(1)}, f32[4,2,128,256]{3,2,1,0:T(8,128)}, u32[]{:S(2)}) copy-start(f32[4,2,128,256]{3,2,1,0:T(8,128)} %get-tuple-element.10) | copy-start | bytes 3145732
  63.7 31.2 %all-to-all-start.1 = ((bf16[32,128,128]{2,1,0:T(8,128)(2,1)}), bf16[32,128,128]{2,1,0:T(8,128)(2,1)S(1)}, u32[]{:S(2)}, u32[]{:S(2)}) async-start(bf16[32,128,128]{2,1,0:T(8,128)(2,1)} %get-tuple-element.12), calls=%async_computation.1 | async-start | bytes 2097152 | tf_op jit(solution)/shard_map/all_to_all | solution.py:337
  69.2 3.2 %collective-permute-start.10 = (bf16[4,2,128,256]{3,2,1,0:T(8,128)(2,1)S(1)}, bf16[4,2,128,256]{3,2,1,0:T(8,128)(2,1)S(1)}, u32[]{:S(2)}, u32[]{:S(2)}) collective-permute-start(bf16[4,2,128,256]{3,2,1,0:T(8,128)(2,1)S(1)} %copy-done.6), channel_id=1, source_target_pairs={{0,1},{1,0},{2,3},{3,2},{4,5},{5,4},{6,7},{7,6},{8,9},{9,8},{10,11... | collective-permute-start | bytes 1572872 | tf_op jit(solution)/shard_map/ppermute | solution.py:332
  72.6 4.8 %collective-permute-start.11 = (bf16[2,128,256]{2,1,0:T(8,128)(2,1)S(1)}, bf16[2,128,256]{2,1,0:T(8,128)(2,1)S(1)}, u32[]{:S(2)}, u32[]{:S(2)}) collective-permute-start(bf16[2,128,256]{2,1,0:T(8,128)(2,1)S(1)} %get-tuple-element.15), channel_id=1, source_target_pairs={{0,2},{2,0},{1,3},{3,1},{4,6},{6,4},{5,7},{7,5},{8,10},{10,8},{9,1... | collective-permute-start | bytes 393224 | tf_op jit(solution)/shard_map/ppermute | solution.py:336
  73.1 8.0 %collective-permute-start.12 = (bf16[2,128,256]{2,1,0:T(8,128)(2,1)S(1)}, bf16[2,128,256]{2,1,0:T(8,128)(2,1)S(1)}, u32[]{:S(2)}, u32[]{:S(2)}) collective-permute-start(bf16[2,128,256]{2,1,0:T(8,128)(2,1)S(1)} %get-tuple-element.17), channel_id=1, source_target_pairs={{0,4},{4,0},{1,5},{5,1},{2,6},{6,2},{3,7},{7,3},{8,12},{12,8},{9,1... | collective-permute-start | bytes 393224 | tf_op jit(solution)/shard_map/ppermute | solution.py:336
  74.9 8.6 %collective-permute-start.13 = (bf16[2,128,256]{2,1,0:T(8,128)(2,1)S(1)}, bf16[2,128,256]{2,1,0:T(8,128)(2,1)S(1)}, u32[]{:S(2)}, u32[]{:S(2)}) collective-permute-start(bf16[2,128,256]{2,1,0:T(8,128)(2,1)S(1)} %get-tuple-element.16), channel_id=1, source_target_pairs={{0,6},{2,4},{4,2},{6,0},{1,7},{3,5},{5,3},{7,1},{8,14},{10,12},{12... | collective-permute-start | bytes 393224 | tf_op jit(solution)/shard_map/ppermute | solution.py:336

commit v3 on v2

--- a/solution.py
+++ b/solution.py
@@ -97,8 +97,8 @@
 def tile_kernel(info, *refs):
     messages, columns = refs[:8], refs[8:12]
     dqmine, dqother, dkv_out = refs[12:15]
-    (qall, kall, dkv, table, order, spos, cum, ks, vs, kst) = refs[15:25]
-    (dks, dvs, lrow, drow, dq, half, sems, done) = refs[25:]
+    (qall, kall, dkv, table, order, rank, spos, cum, ks, vs, kst) = refs[15:26]
+    (dks, dvs, lrow, drow, dq, half, sems, done) = refs[26:]
     key_copies = fetch(columns, [kall.at[pl.ds(8 * c, 8)] for c in range(4)], sems)
     slots = (0, 2, 4, 6, 1, 3, 5, 7)
     copies = [None] * 8
@@ -123,6 +123,7 @@
     def scan(p, count):
         i = table[p]
         order[count] = i
+        rank[jnp.where(i >= 0, i, BLOCKS)] = count
         spos[count] = p
         count = count + jnp.where(i >= 0, 1, 0)
         cum[p] = count
@@ -238,22 +239,29 @@
 
     lax.fori_loop(0, 4, half_block, 0)
 
-    def restore(r, _):
-        i = order[r]
-        dst = pl.multiple_of((i % 2) * PART, PART)
-        src = pl.multiple_of(r * PART, PART)
-        shard = i // 2 % 8 * 4 + (i // 16 + x) % 4
-        dkv[shard, pl.ds(dst, PART), :] = dks[pl.ds(src, PART), :].astype(jnp.bfloat16)
-        dkv[shard, pl.ds(dst + 2 * PART, PART), :] = dvs[pl.ds(src, PART), :].astype(jnp.bfloat16)
-        return 0
-
-    lax.fori_loop(0, BLOCKS, restore, 0, unroll=8)
-    copy = pltpu.make_async_copy(dkv, dkv_out, sems.at[0])
-    copy.start()
+    back = []
+    for c in range(4):
+
+        def restore(i, _):
+            src = pl.multiple_of(rank[i] * PART, PART)
+            dst = pl.multiple_of((i % 2) * PART, PART)
+            shard = i // 2
+            dkv[shard, pl.ds(dst, PART), :] = dks[pl.ds(src, PART), :].astype(jnp.bfloat16)
+            dkv[shard, pl.ds(dst + 2 * PART, PART), :] = dvs[pl.ds(src, PART), :].astype(jnp.bfloat16)
+            return 0
+
+        lax.fori_loop(16 * c, 16 * c + 16, restore, 0, unroll=8)
+        back.append(
+            pltpu.make_async_copy(
+                dkv.at[pl.ds(8 * c, 8)], dkv_out.at[:, (x + c) % 4], sems.at[c]
+            )
+        )
+        back[-1].start()
     for hb4 in range(4):
         for piece in dq_out(hb4):
             piece.wait()
-    copy.wait()
+    for copy in back:
+        copy.wait()
 
 
 VMEM = pl.BlockSpec(memory_space=pltpu.VMEM)
@@ -280,7 +288,7 @@
         out_shape=(
             jax.ShapeDtypeStruct((4, 2, DH, 2 * HALF), jnp.float32),
             jax.ShapeDtypeStruct((4, 2, DH, 2 * HALF), jnp.bfloat16),
-            jax.ShapeDtypeStruct((SHARDS, 4 * PART, DH), jnp.bfloat16),
+            jax.ShapeDtypeStruct((8, 4, 4 * PART, DH), jnp.bfloat16),
         ),
         in_specs=[SMEM] + [HBM] * 12,
         out_specs=(HBM, HBM, HBM),
@@ -288,6 +296,7 @@
             pltpu.VMEM((8, QROWS, DH), jnp.bfloat16),
             pltpu.VMEM((SHARDS, KROWS, DH), jnp.bfloat16),
             pltpu.VMEM((SHARDS, 4 * PART, DH), jnp.bfloat16),
+            pltpu.SMEM((2 * BLOCKS,), jnp.int32),
             pltpu.SMEM((2 * BLOCKS,), jnp.int32),
             pltpu.SMEM((2 * BLOCKS,), jnp.int32),
             pltpu.SMEM((2 * BLOCKS,), jnp.int32),
@@ -318,10 +327,11 @@
     kmsg = pack(pack_keys_kernel, (8, KROWS, DH), block_pos, key_rows, head_value_rows)
     qmsg = pack(pack_queries_kernel, (QROWS, DH), block_pos, query, out_grad, output, logsumexp)
     column = lax.all_to_all(kmsg, "z", 0, 0, tiled=True)
+    early = lax.ppermute(qmsg, *STEPS[1])
     column, qmsg = lax.optimization_barrier((column, qmsg))
     columns = [column] + [lax.ppermute(column, "x", moved(-d, 4)) for d in (2, 1, 3)]
     columns = [columns[0], columns[2], columns[1], columns[3]]
-    near = [qmsg] + [lax.ppermute(qmsg, axes, route) for axes, route in STEPS]
+    near = [qmsg, lax.ppermute(qmsg, *STEPS[0]), early, lax.ppermute(qmsg, *STEPS[2])]
     far = [lax.ppermute(message, "core", SWAP) for message in near]
 
     places = [c[:, 4 * PART, :2].reshape(16) for c in columns]
@@ -334,6 +344,7 @@
     dq = dq[0]
     for i, (axes, route) in enumerate(STEPS):
         dq = dq + lax.ppermute(low[i + 1], axes, route).astype(jnp.float32)
+    dkv = dkv.reshape(SHARDS, 4 * PART, DH)
     dkv = lax.all_to_all(dkv, KEY_GROUP, 0, 0, tiled=True)
     total = jnp.sum(dkv.astype(jnp.float32), axis=0)
     factor = jnp.where(jnp.arange(4 * PART) < 2 * PART, SCALE, 1.0).astype(jnp.float32)

time: 105 us -> 102 us (0.971)
  waiting for transfers between devices: 34.1 us -> 27.4 us
  starting transfers between devices: 33.2 us -> 37.2 us
    ppermute x3, waiting for transfers between devices: 6.31 us -> 1.9 us  [the longest x1 1.89 us: shards(): lax.ppermute(qmsg, *STEPS[0])]
    all_to_all x1, waiting for transfers between devices: 8.59 us -> 5.58 us  [shards(): column = lax.all_to_all(kmsg, 'z', 0, 0, tiled=True)]
    ppermute x3, starting transfers between devices: 3.69 us -> 6.2 us  [the longest x1 3 us: shards(): early = lax.ppermute(qmsg, *STEPS[1])]
    ppermute x4, starting transfers between devices: 5.2 us -> 7.68 us  [shards(): far = [lax.ppermute(message, 'core', SWAP) for message in near]]
    ppermute x3, waiting for transfers between devices: 6.97 us -> 8.53 us  [shards(): dq = dq + lax.ppermute(low[i + 1], axes, route).astype(jnp.float32)]
    all_to_all x1, waiting for transfers between devices: 10.5 us -> 9.21 us  [shards(): dkv = lax.all_to_all(dkv, KEY_GROUP, 0, 0, tiled=True)]
  transfers between devices with their start and end apart: 16 -> 16, of which waited for: 10 -> 8; matrix products, arithmetic and copies ran while one was open for 2% -> 2% of each run, Pallas kernels for 2% -> 3%
where the time goes in v3:
time: 102 us; the launch traced here: 101 us
  starting transfers between devices  37.2 us (36%)
  waiting for transfers between devices  27.4 us (27%)
  Pallas kernels  22.4 us (22%)
  blocking collectives  8.33 us (8%)
  local copies, waits for them, and re-layouts  4.25 us (4%)
    pallas_call x1, Pallas kernels, tile(): pl.pallas_call(tile_kernel, out_shape=(jax.ShapeDtypeStruct((4, 2, DH, 2...  17.4 us
    all_to_all x1, waiting for transfers between devices, shards(): dkv = lax.all_to_all(dkv, KEY_GROUP, 0, 0, tiled=True)  9.21 us
    all_to_all x1, starting transfers between devices, shards(): column = lax.all_to_all(kmsg, 'z', 0, 0, tiled=True)  9.03 us
    ppermute x3, waiting for transfers between devices, shards(): dq = dq + lax.ppermute(low[i + 1], axes, route).astype(jnp.float32)  8.53 us
    all_gather x1, blocking collectives, shards(): quarters = lax.all_gather(mine, HEADS, tiled=False)  8.33 us
    ppermute x4, starting transfers between devices, shards(): far = [lax.ppermute(message, 'core', SWAP) for message in near]  7.68 us
    all_to_all x1, waiting for transfers between devices, shards(): column = lax.all_to_all(kmsg, 'z', 0, 0, tiled=True)  5.58 us
    all_to_all x1, starting transfers between devices, shards(): dkv = lax.all_to_all(dkv, KEY_GROUP, 0, 0, tiled=True)  5.21 us
  transfers between devices with their start and end apart: 16, of which 8 were waited for; matrix products, arithmetic and copies ran while one was open for 2% of the time, Pallas kernels for 3%

profile of v3, /device:TPU:1, one launch (start us, length us, event | category | flops | bytes accessed | tf_op | source)
XLA Modules:
  0.0 101.4 jit_solution(7512426645857154864)
XLA Ops:
  0.6 0.0 copy-start.2
  0.6 2.4 %pack.2 = bf16[8,144,128]{2,1,0:T(8,128)(2,1)} custom-call(s32[2]{0:T(128)} %block_pos.3, bf16[256,128]{1,0:T(8,128)(2,1)} %key_in.1, bf16[256,128]{1,0:T(8,128)(2,1)} %value_in.1), custom_call_target="tpu_custom_call" | custom-call | tf_op jit(solution)/shard_map/pack/pallas_call | solution.py:273
  3.1 9.0 %all-to-all-start = ((bf16[8,144,128]{2,1,0:T(8,128)(2,1)}), bf16[8,144,128]{2,1,0:T(8,128)(2,1)S(1)}, u32[]{:S(2)}, u32[]{:S(2)}) async-start(bf16[8,144,128]{2,1,0:T(8,128)(2,1)} %pack.2), calls=%async_computation | async-start | bytes 589824 | tf_op jit(solution)/shard_map/all_to_all | solution.py:329
  12.1 2.6 %pack.3.refs_0_ = bf16[1056,128]{1,0:T(8,128)(2,1)} custom-call(s32[2]{0:T(128)} %block_pos.3, bf16[256,256]{1,0:T(8,128)(2,1)} %refs_0_.1, bf16[256,256]{1,0:T(8,128)(2,1)} %refs_1_.1, bf16[256,256]{1,0:T(8,128)(2,1)} %refs_2_.1, f32[2,256]{1,0:T(2,128)} %refs_3_.1), custom_call_target="tpu_custom_call" | custom-call | tf_op jit(solution)/shard_map/pack/pallas_call | solution.py:273
  14.7 3.0 %collective-permute-start.3 = (bf16[1056,128]{1,0:T(8,128)(2,1)}, bf16[1056,128]{1,0:T(8,128)(2,1)S(1)}, u32[]{:S(2)}, u32[]{:S(2)}) collective-permute-start(bf16[1056,128]{1,0:T(8,128)(2,1)} %pack.3.refs_0_), channel_id=1, source_target_pairs={{0,4},{4,0},{1,5},{5,1},{2,6},{6,2},{3,7},{7,3},{8,12},{12,8},{9,1... | collective-permute-start | bytes 811016 | tf_op jit(solution)/shard_map/ppermute | solution.py:330
  17.7 0.0 copy-done.2
  17.7 5.6 %all-to-all-done.refs_8_ = bf16[8,144,128]{2,1,0:T(8,128)(2,1)S(1)} async-done(((bf16[8,144,128]{2,1,0:T(8,128)(2,1)}), bf16[8,144,128]{2,1,0:T(8,128)(2,1)S(1)}, u32[]{:S(2)}, u32[]{:S(2)}) %all-to-all-start) | async-done | bytes 294944 | tf_op jit(solution)/shard_map/all_to_all | solution.py:329
  23.3 2.5 %collective-permute-start = (bf16[8,144,128]{2,1,0:T(8,128)(2,1)S(1)}, bf16[8,144,128]{2,1,0:T(8,128)(2,1)S(1)}, u32[]{:S(2)}, u32[]{:S(2)}) collective-permute-start(bf16[8,144,128]{2,1,0:T(8,128)(2,1)S(1)} %all-to-all-done.refs_8_), channel_id=1, source_target_pairs={{0,24},{8,0},{16,8},{24,16},{1,25},{9,1},{17,9},{25,17},{2,26},{10... | collective-permute-start | bytes 884744 | tf_op jit(solution)/shard_map/ppermute | solution.py:332
  25.8 0.5 collective-permute-start.1
  26.3 1.3 %collective-permute-start.4 = (bf16[1056,128]{1,0:T(8,128)(2,1)}, bf16[1056,128]{1,0:T(8,128)(2,1)S(1)}, u32[]{:S(2)}, u32[]{:S(2)}) collective-permute-start(bf16[1056,128]{1,0:T(8,128)(2,1)} %pack.3.refs_0_), channel_id=1, source_target_pairs={{0,2},{2,0},{1,3},{3,1},{4,6},{6,4},{5,7},{7,5},{8,10},{10,8},{9,1... | collective-permute-start | bytes 811016 | tf_op jit(solution)/shard_map/ppermute | solution.py:334
  27.6 1.9 %collective-permute-start.5 = (bf16[1056,128]{1,0:T(8,128)(2,1)}, bf16[1056,128]{1,0:T(8,128)(2,1)S(1)}, u32[]{:S(2)}, u32[]{:S(2)}) collective-permute-start(bf16[1056,128]{1,0:T(8,128)(2,1)} %pack.3.refs_0_), channel_id=1, source_target_pairs={{0,6},{2,4},{4,2},{6,0},{1,7},{3,5},{5,3},{7,1},{8,14},{10,12},{12... | collective-permute-start | bytes 811016 | tf_op jit(solution)/shard_map/ppermute | solution.py:334
  29.5 0.0 collective-permute-done.3.refs_2_
  29.5 0.6 collective-permute-start.2
  30.1 0.1 reshape_squeeze.12
  30.2 1.9 %collective-permute-done.4.refs_1_ = bf16[1056,128]{1,0:T(8,128)(2,1)S(1)} collective-permute-done((bf16[1056,128]{1,0:T(8,128)(2,1)}, bf16[1056,128]{1,0:T(8,128)(2,1)S(1)}, u32[]{:S(2)}, u32[]{:S(2)}) %collective-permute-start.4) | collective-permute-done | bytes 270368 | tf_op jit(solution)/shard_map/ppermute | solution.py:334
  32.1 3.8 %collective-permute-start.8 = (bf16[1056,128]{1,0:T(8,128)(2,1)S(1)}, bf16[1056,128]{1,0:T(8,128)(2,1)S(1)}, u32[]{:S(2)}, u32[]{:S(2)}) collective-permute-start(bf16[1056,128]{1,0:T(8,128)(2,1)S(1)} %collective-permute-done.3.refs_2_), channel_id=1, source_target_pairs={{0,1},{1,0},{2,3},{3,2},{4,5},{5,4},{6,7},{7,6},{8,9},{9,8},{10,11... | collective-permute-start | bytes 811016 | tf_op jit(solution)/shard_map/ppermute | solution.py:335
  35.9 0.0 collective-permute-done.5.refs_3_
  35.9 2.8 %collective-permute-start.6 = (bf16[1056,128]{1,0:T(8,128)(2,1)}, bf16[1056,128]{1,0:T(8,128)(2,1)S(1)}, u32[]{:S(2)}, u32[]{:S(2)}) collective-permute-start(bf16[1056,128]{1,0:T(8,128)(2,1)} %pack.3.refs_0_), channel_id=1, source_target_pairs={{0,1},{1,0},{2,3},{3,2},{4,5},{5,4},{6,7},{7,6},{8,9},{9,8},{10,11... | collective-permute-start | bytes 811016 | tf_op jit(solution)/shard_map/ppermute | solution.py:335
  38.7 0.0 collective-permute-done.refs_9_
  38.7 0.7 collective-permute-start.7
  39.3 0.0 collective-permute-done.1.refs_10_
  39.3 0.5 collective-permute-start.9
  39.8 0.1 reshape_squeeze.13
  39.9 0.1 reshape_squeeze.14
  40.0 0.7 collective-permute-done.2.refs_11_
  40.7 0.1 reshape_squeeze.15
  40.8 0.1 concatenate.3
  40.9 0.5 convert_element_type.47.info
  41.4 0.0 collective-permute-done.8.refs_6_
  41.4 0.0 collective-permute-done.6.refs_4_
  41.4 0.0 copy-start.11
  41.4 0.0 collective-permute-done.7.refs_5_
  41.5 0.0 copy-start.12
  41.5 0.0 collective-permute-done.9.refs_7_
  41.5 0.0 copy-done.1
  41.5 0.0 copy-done.7
  41.5 0.0 copy-done.8
  41.5 0.0 copy-done.9
  41.5 0.0 copy-done.3
  41.5 0.0 copy-done.4
  41.5 0.6 copy-done.10
  42.1 0.1 copy-done.11
  42.2 0.1 copy-done.12
  42.4 0.7 copy-done.13
  43.1 17.4 %tile.1 = (f32[4,2,128,256]{3,2,1,0:T(8,128)}, bf16[4,2,128,256]{3,2,1,0:T(8,128)(2,1)}, bf16[8,4,128,128]{3,2,1,0:T(8,128)(2,1)}) custom-call(s32[68]{0:T(128)} %convert_element_type.47.info, bf16[1056,128]{1,0:T(8,128)(2,1)} %pack.3.refs_0_, bf16[1056,128]{1,0:T(8,128)(2,1)} %copy-done.8, bf16[1056,128]{1,0:T(8,128)(2,1)} %copy-done.7, ...), custom_call_target="tpu_custom_call" | custom-call | flops 6000000000 | bytes 6291456 | tf_op jit(solution)/shard_map/tile/pallas_call | solution.py:286
  60.4 5.2 %all-to-all-start.1 = ((bf16[32,128,128]{2,1,0:T(8,128)(2,1)}), bf16[32,128,128]{2,1,0:T(8,128)(2,1)S(1)}, u32[]{:S(2)}, u32[]{:S(2)}) async-start(bf16[32,128,128]{2,1,0:T(8,128)(2,1)} %bitcast.36), calls=%async_computation.1 | async-start | bytes 2097152 | tf_op jit(solution)/shard_map/all_to_all | solution.py:348
  65.7 1.6 %collective-permute-start.10 = (bf16[4,2,128,256]{3,2,1,0:T(8,128)(2,1)S(1)}, bf16[4,2,128,256]{3,2,1,0:T(8,128)(2,1)S(1)}, u32[]{:S(2)}, u32[]{:S(2)}) collective-permute-start(bf16[4,2,128,256]{3,2,1,0:T(8,128)(2,1)S(1)} %copy-done.6), channel_id=1, source_target_pairs={{0,1},{1,0},{2,3},{3,2},{4,5},{5,4},{6,7},{7,6},{8,9},{9,8},{10,11... | collective-permute-start | bytes 1572872 | tf_op jit(solution)/shard_map/ppermute | solution.py:342
  67.2 1.5 %collective-permute-done.10 = bf16[4,2,128,256]{3,2,1,0:T(8,128)(2,1)S(1)} collective-permute-done((bf16[4,2,128,256]{3,2,1,0:T(8,128)(2,1)S(1)}, bf16[4,2,128,256]{3,2,1,0:T(8,128)(2,1)S(1)}, u32[]{:S(2)}, u32[]{:S(2)}) %collective-permute-start.10) | collective-permute-done | bytes 524320 | tf_op jit(solution)/shard_map/ppermute | solution.py:342
  68.8 0.2 fusion.6
  69.0 1.3 %collective-permute-start.11 = (bf16[2,128,256]{2,1,0:T(8,128)(2,1)S(1)}, bf16[2,128,256]{2,1,0:T(8,128)(2,1)S(1)}, u32[]{:S(2)}, u32[]{:S(2)}) collective-permute-start(bf16[2,128,256]{2,1,0:T(8,128)(2,1)S(1)} %get-tuple-element.15), channel_id=1, source_target_pairs={{0,2},{2,0},{1,3},{3,1},{4,6},{6,4},{5,7},{7,5},{8,10},{10,8},{9,1... | collective-permute-start | bytes 393224 | tf_op jit(solution)/shard_map/ppermute | solution.py:346
  70.3 2.6 %collective-permute-start.12 = (bf16[2,128,256]{2,1,0:T(8,128)(2,1)S(1)}, bf16[2,128,256]{2,1,0:T(8,128)(2,1)S(1)}, u32[]{:S(2)}, u32[]{:S(2)}) collective-permute-start(bf16[2,128,256]{2,1,0:T(8,128)(2,1)S(1)} %get-tuple-element.17), channel_id=1, source_target_pairs={{0,4},{4,0},{1,5},{5,1},{2,6},{6,2},{3,7},{7,3},{8,12},{12,8},{9,1... | collective-permute-start | bytes 393224 | tf_op jit(solution)/shard_map/ppermute | solution.py:346
  72.9 0.1 collective-permute-start.13
  72.9 0.8 collective-permute-done.11
  73.8 5.2 %collective-permute-done.12 = bf16[2,128,256]{2,1,0:T(8,128)(2,1)S(1)} collective-permute-done((bf16[2,128,256]{2,1,0:T(8,128)(2,1)S(1)}, bf16[2,128,256]{2,1,0:T(8,128)(2,1)S(1)}, u32[]{:S(2)}, u32[]{:S(2)}) %collective-permute-start.12) | collective-permute-done | bytes 131104 | tf_op jit(solution)/shard_map/ppermute | solution.py:346
  79.0 2.5 %collective-permute-done.13 = bf16[2,128,256]{2,1,0:T(8,128)(2,1)S(1)} collective-permute-done((bf16[2,128,256]{2,1,0:T(8,128)(2,1)S(1)}, bf16[2,128,256]{2,1,0:T(8,128)(2,1)S(1)}, u32[]{:S(2)}, u32[]{:S(2)}) %collective-permute-start.13) | collective-permute-done | bytes 131104 | tf_op jit(solution)/shard_map/ppermute | solution.py:346
  81.5 0.1 fusion.4
  81.6 0.1 copy.15
  81.7 0.7 copy.20
  82.4 9.2 %all-to-all-done.1 = bf16[32,128,128]{2,1,0:T(8,128)(2,1)S(1)} async-done(((bf16[32,128,128]{2,1,0:T(8,128)(2,1)}), bf16[32,128,128]{2,1,0:T(8,128)(2,1)S(1)}, u32[]{:S(2)}, u32[]{:S(2)}) %all-to-all-start.1) | async-done | bytes 1048608 | tf_op jit(solution)/shard_map/all_to_all | solution.py:348
  91.6 0.2 convert_reduce_fusion
  91.7 0.1 fusion.5
  91.8 8.3 %all_gather.4 = bf16[4,128,128]{2,1,0:T(8,128)(2,1)S(1)} all-gather(bf16[1,128,128]{2,1,0:T(8,128)(2,1)S(1)} %fusion.5), channel_id=1, replica_groups=mesh['z'=8,'x'=4,'yh'=2,'yl'=2,'core'=2] {'yl','core'}, dimensions={0}, use_global_device_ids=true | all-gather | bytes 163840 | tf_op jit(solution)/shard_map/all_gather | solution.py:352
  100.2 0.6 copy.16
  100.8 0.6 copy.17
  (24 shorter events, 0.2 us)
Async XLA Ops:
  0.6 17.1 %copy-start.2 = (s32[2]{0:T(128)S(1)}, s32[2]{0:T(128)}, u32[]{:S(2)}) copy-start(s32[2]{0:T(128)} %block_pos.3) | copy-start | bytes 28
  3.1 20.2 %all-to-all-start = ((bf16[8,144,128]{2,1,0:T(8,128)(2,1)}), bf16[8,144,128]{2,1,0:T(8,128)(2,1)S(1)}, u32[]{:S(2)}, u32[]{:S(2)}) async-start(bf16[8,144,128]{2,1,0:T(8,128)(2,1)} %pack.2), calls=%async_computation | async-start | bytes 589824 | tf_op jit(solution)/shard_map/all_to_all | solution.py:329
  14.7 14.8 %collective-permute-start.3 = (bf16[1056,128]{1,0:T(8,128)(2,1)}, bf16[1056,128]{1,0:T(8,128)(2,1)S(1)}, u32[]{:S(2)}, u32[]{:S(2)}) collective-permute-start(bf16[1056,128]{1,0:T(8,128)(2,1)} %pack.3.refs_0_), channel_id=1, source_target_pairs={{0,4},{4,0},{1,5},{5,1},{2,6},{6,2},{3,7},{7,3},{8,12},{12,8},{9,1... | collective-permute-start | bytes 811016 | tf_op jit(solution)/shard_map/ppermute | solution.py:330
  23.3 18.2 %copy-start.1 = (bf16[8,144,128]{2,1,0:T(8,128)(2,1)}, bf16[8,144,128]{2,1,0:T(8,128)(2,1)S(1)}, u32[]{:S(2)}) copy-start(bf16[8,144,128]{2,1,0:T(8,128)(2,1)S(1)} %all-to-all-done.refs_8_) | copy-start | bytes 884740
  23.3 15.4 %collective-permute-start = (bf16[8,144,128]{2,1,0:T(8,128)(2,1)S(1)}, bf16[8,144,128]{2,1,0:T(8,128)(2,1)S(1)}, u32[]{:S(2)}, u32[]{:S(2)}) collective-permute-start(bf16[8,144,128]{2,1,0:T(8,128)(2,1)S(1)} %all-to-all-done.refs_8_), channel_id=1, source_target_pairs={{0,24},{8,0},{16,8},{24,16},{1,25},{9,1},{17,9},{25,17},{2,26},{10... | collective-permute-start | bytes 884744 | tf_op jit(solution)/shard_map/ppermute | solution.py:332
  25.8 13.6 %collective-permute-start.1 = (bf16[8,144,128]{2,1,0:T(8,128)(2,1)S(1)}, bf16[8,144,128]{2,1,0:T(8,128)(2,1)S(1)}, u32[]{:S(2)}, u32[]{:S(2)}) collective-permute-start(bf16[8,144,128]{2,1,0:T(8,128)(2,1)S(1)} %all-to-all-done.refs_8_), channel_id=1, source_target_pairs={{0,16},{8,24},{16,0},{24,8},{1,17},{9,25},{17,1},{25,9},{2,18},{10... | collective-permute-start | bytes 884744 | tf_op jit(solution)/shard_map/ppermute | solution.py:332
  26.3 5.8 %collective-permute-start.4 = (bf16[1056,128]{1,0:T(8,128)(2,1)}, bf16[1056,128]{1,0:T(8,128)(2,1)S(1)}, u32[]{:S(2)}, u32[]{:S(2)}) collective-permute-start(bf16[1056,128]{1,0:T(8,128)(2,1)} %pack.3.refs_0_), channel_id=1, source_target_pairs={{0,2},{2,0},{1,3},{3,1},{4,6},{6,4},{5,7},{7,5},{8,10},{10,8},{9,1... | collective-permute-start | bytes 811016 | tf_op jit(solution)/shard_map/ppermute | solution.py:334
  27.6 8.3 %collective-permute-start.5 = (bf16[1056,128]{1,0:T(8,128)(2,1)}, bf16[1056,128]{1,0:T(8,128)(2,1)S(1)}, u32[]{:S(2)}, u32[]{:S(2)}) collective-permute-start(bf16[1056,128]{1,0:T(8,128)(2,1)} %pack.3.refs_0_), channel_id=1, source_target_pairs={{0,6},{2,4},{4,2},{6,0},{1,7},{3,5},{5,3},{7,1},{8,14},{10,12},{12... | collective-permute-start | bytes 811016 | tf_op jit(solution)/shard_map/ppermute | solution.py:334
  29.5 12.0 %copy-start.7 = (bf16[1056,128]{1,0:T(8,128)(2,1)}, bf16[1056,128]{1,0:T(8,128)(2,1)S(1)}, u32[]{:S(2)}) copy-start(bf16[1056,128]{1,0:T(8,128)(2,1)S(1)} %collective-permute-done.3.refs_2_) | copy-start | bytes 811012
  29.5 11.2 %collective-permute-start.2 = (bf16[8,144,128]{2,1,0:T(8,128)(2,1)S(1)}, bf16[8,144,128]{2,1,0:T(8,128)(2,1)S(1)}, u32[]{:S(2)}, u32[]{:S(2)}) collective-permute-start(bf16[8,144,128]{2,1,0:T(8,128)(2,1)S(1)} %all-to-all-done.refs_8_), channel_id=1, source_target_pairs={{0,8},{8,16},{16,24},{24,0},{1,9},{9,17},{17,25},{25,1},{2,10},{10... | collective-permute-start | bytes 884744 | tf_op jit(solution)/shard_map/ppermute | solution.py:332
  32.1 9.4 %copy-start.8 = (bf16[1056,128]{1,0:T(8,128)(2,1)}, bf16[1056,128]{1,0:T(8,128)(2,1)S(1)}, u32[]{:S(2)}) copy-start(bf16[1056,128]{1,0:T(8,128)(2,1)S(1)} %collective-permute-done.4.refs_1_) | copy-start | bytes 811012
  32.1 9.3 %collective-permute-start.8 = (bf16[1056,128]{1,0:T(8,128)(2,1)S(1)}, bf16[1056,128]{1,0:T(8,128)(2,1)S(1)}, u32[]{:S(2)}, u32[]{:S(2)}) collective-permute-start(bf16[1056,128]{1,0:T(8,128)(2,1)S(1)} %collective-permute-done.3.refs_2_), channel_id=1, source_target_pairs={{0,1},{1,0},{2,3},{3,2},{4,5},{5,4},{6,7},{7,6},{8,9},{9,8},{10,11... | collective-permute-start | bytes 811016 | tf_op jit(solution)/shard_map/ppermute | solution.py:335
  35.9 5.6 %copy-start.9 = (bf16[1056,128]{1,0:T(8,128)(2,1)}, bf16[1056,128]{1,0:T(8,128)(2,1)S(1)}, u32[]{:S(2)}) copy-start(bf16[1056,128]{1,0:T(8,128)(2,1)S(1)} %collective-permute-done.5.refs_3_) | copy-start | bytes 811012
  35.9 5.5 %collective-permute-start.6 = (bf16[1056,128]{1,0:T(8,128)(2,1)}, bf16[1056,128]{1,0:T(8,128)(2,1)S(1)}, u32[]{:S(2)}, u32[]{:S(2)}) collective-permute-start(bf16[1056,128]{1,0:T(8,128)(2,1)} %pack.3.refs_0_), channel_id=1, source_target_pairs={{0,1},{1,0},{2,3},{3,2},{4,5},{5,4},{6,7},{7,6},{8,9},{9,8},{10,11... | collective-permute-start | bytes 811016 | tf_op jit(solution)/shard_map/ppermute | solution.py:335
  38.7 2.8 %copy-start.3 = (bf16[8,144,128]{2,1,0:T(8,128)(2,1)}, bf16[8,144,128]{2,1,0:T(8,128)(2,1)S(1)}, u32[]{:S(2)}) copy-start(bf16[8,144,128]{2,1,0:T(8,128)(2,1)S(1)} %collective-permute-done.refs_9_) | copy-start | bytes 884740
  38.7 2.8 %collective-permute-start.7 = (bf16[1056,128]{1,0:T(8,128)(2,1)S(1)}, bf16[1056,128]{1,0:T(8,128)(2,1)S(1)}, u32[]{:S(2)}, u32[]{:S(2)}) collective-permute-start(bf16[1056,128]{1,0:T(8,128)(2,1)S(1)} %collective-permute-done.4.refs_1_), channel_id=1, source_target_pairs={{0,1},{1,0},{2,3},{3,2},{4,5},{5,4},{6,7},{7,6},{8,9},{9,8},{10,11... | collective-permute-start | bytes 811016 | tf_op jit(solution)/shard_map/ppermute | solution.py:335
  39.3 2.2 %copy-start.4 = (bf16[8,144,128]{2,1,0:T(8,128)(2,1)}, bf16[8,144,128]{2,1,0:T(8,128)(2,1)S(1)}, u32[]{:S(2)}) copy-start(bf16[8,144,128]{2,1,0:T(8,128)(2,1)S(1)} %collective-permute-done.1.refs_10_) | copy-start | bytes 884740
  39.3 2.1 %collective-permute-start.9 = (bf16[1056,128]{1,0:T(8,128)(2,1)S(1)}, bf16[1056,128]{1,0:T(8,128)(2,1)S(1)}, u32[]{:S(2)}, u32[]{:S(2)}) collective-permute-start(bf16[1056,128]{1,0:T(8,128)(2,1)S(1)} %collective-permute-done.5.refs_3_), channel_id=1, source_target_pairs={{0,1},{1,0},{2,3},{3,2},{4,5},{5,4},{6,7},{7,6},{8,9},{9,8},{10,11... | collective-permute-start | bytes 811016 | tf_op jit(solution)/shard_map/ppermute | solution.py:335
  40.7 0.9 copy-start.5
  41.4 0.7 copy-start.10
  41.4 0.8 copy-start.11
  41.5 0.9 copy-start.12
  42.4 0.7 copy-start.13
  60.4 5.2 %copy-start.6 = (bf16[4,2,128,256]{3,2,1,0:T(8,128)(2,1)S(1)}, bf16[4,2,128,256]{3,2,1,0:T(8,128)(2,1)}, u32[]{:S(2)}) copy-start(bf16[4,2,128,256]{3,2,1,0:T(8,128)(2,1)} %get-tuple-element.11) | copy-start | bytes 1572868
  60.4 8.3 %copy-start = (f32[4,2,128,256]{3,2,1,0:T(8,128)S(1)}, f32[4,2,128,256]{3,2,1,0:T(8,128)}, u32[]{:S(2)}) copy-start(f32[4,2,128,256]{3,2,1,0:T(8,128)} %get-tuple-element.10) | copy-start | bytes 3145732
  60.4 31.1 %all-to-all-start.1 = ((bf16[32,128,128]{2,1,0:T(8,128)(2,1)}), bf16[32,128,128]{2,1,0:T(8,128)(2,1)S(1)}, u32[]{:S(2)}, u32[]{:S(2)}) async-start(bf16[32,128,128]{2,1,0:T(8,128)(2,1)} %bitcast.36), calls=%async_computation.1 | async-start | bytes 2097152 | tf_op jit(solution)/shard_map/all_to_all | solution.py:348
  65.7 3.1 %collective-permute-start.10 = (bf16[4,2,128,256]{3,2,1,0:T(8,128)(2,1)S(1)}, bf16[4,2,128,256]{3,2,1,0:T(8,128)(2,1)S(1)}, u32[]{:S(2)}, u32[]{:S(2)}) collective-permute-start(bf16[4,2,128,256]{3,2,1,0:T(8,128)(2,1)S(1)} %copy-done.6), channel_id=1, source_target_pairs={{0,1},{1,0},{2,3},{3,2},{4,5},{5,4},{6,7},{7,6},{8,9},{9,8},{10,11... | collective-permute-start | bytes 1572872 | tf_op jit(solution)/shard_map/ppermute | solution.py:342
  69.0 4.8 %collective-permute-start.11 = (bf16[2,128,256]{2,1,0:T(8,128)(2,1)S(1)}, bf16[2,128,256]{2,1,0:T(8,128)(2,1)S(1)}, u32[]{:S(2)}, u32[]{:S(2)}) collective-permute-start(bf16[2,128,256]{2,1,0:T(8,128)(2,1)S(1)} %get-tuple-element.15), channel_id=1, source_target_pairs={{0,2},{2,0},{1,3},{3,1},{4,6},{6,4},{5,7},{7,5},{8,10},{10,8},{9,1... | collective-permute-start | bytes 393224 | tf_op jit(solution)/shard_map/ppermute | solution.py:346
  70.3 8.7 %collective-permute-start.12 = (bf16[2,128,256]{2,1,0:T(8,128)(2,1)S(1)}, bf16[2,128,256]{2,1,0:T(8,128)(2,1)S(1)}, u32[]{:S(2)}, u32[]{:S(2)}) collective-permute-start(bf16[2,128,256]{2,1,0:T(8,128)(2,1)S(1)} %get-tuple-element.17), channel_id=1, source_target_pairs={{0,4},{4,0},{1,5},{5,1},{2,6},{6,2},{3,7},{7,3},{8,12},{12,8},{9,1... | collective-permute-start | bytes 393224 | tf_op jit(solution)/shard_map/ppermute | solution.py:346
  72.9 8.6 %collective-permute-start.13 = (bf16[2,128,256]{2,1,0:T(8,128)(2,1)S(1)}, bf16[2,128,256]{2,1,0:T(8,128)(2,1)S(1)}, u32[]{:S(2)}, u32[]{:S(2)}) collective-permute-start(bf16[2,128,256]{2,1,0:T(8,128)(2,1)S(1)} %get-tuple-element.16), channel_id=1, source_target_pairs={{0,6},{2,4},{4,2},{6,0},{1,7},{3,5},{5,3},{7,1},{8,14},{10,12},{12... | collective-permute-start | bytes 393224 | tf_op jit(solution)/shard_map/ppermute | solution.py:346

commit v4 on v3

--- a/solution.py
+++ b/solution.py
@@ -24,7 +24,7 @@
 BLOCKS = 2 * SHARDS
 KEYS = BLOCKS * PART
 QROWS = 4 * HALF * 2 + 32
-KROWS = 4 * PART + 16
+KROWS = 4 * PART + 8
 SPAN = 8
 CHUNK = SPAN * PART
 VMEM_BYTES = 60 << 20
@@ -55,8 +55,7 @@
 
 def pack_keys_kernel(block_pos, key_in, value_in, kmsg, key, value, sems):
     copies = fetch((key_in, value_in), (key, value), sems)
-    places = place_row(block_pos)
-    places = jnp.concatenate([places, places], axis=0).astype(jnp.bfloat16)
+    places = place_row(block_pos).astype(jnp.bfloat16)
     quarter = lax.axis_index(HEADS)
     block = []
     for array, copy in zip((key, value), copies):
@@ -97,8 +96,8 @@
 def tile_kernel(info, *refs):
     messages, columns = refs[:8], refs[8:12]
     dqmine, dqother, dkv_out = refs[12:15]
-    (qall, kall, dkv, table, order, rank, spos, cum, ks, vs, kst) = refs[15:26]
-    (dks, dvs, lrow, drow, dq, half, sems, done) = refs[26:]
+    (qall, kall, dkv, table, rank, spos, cum, ks, vs, kst) = refs[15:25]
+    (dks, dvs, lrow, drow, dq, half, sems, done) = refs[25:]
     key_copies = fetch(columns, [kall.at[pl.ds(8 * c, 8)] for c in range(4)], sems)
     slots = (0, 2, 4, 6, 1, 3, 5, 7)
     copies = [None] * 8
@@ -122,7 +121,6 @@
 
     def scan(p, count):
         i = table[p]
-        order[count] = i
         rank[jnp.where(i >= 0, i, BLOCKS)] = count
         spos[count] = p
         count = count + jnp.where(i >= 0, 1, 0)
@@ -133,18 +131,17 @@
     dks[...] = jnp.zeros_like(dks)
     dvs[...] = jnp.zeros_like(dvs)
     dq[...] = jnp.zeros_like(dq)
-    for copy in key_copies:
-        copy.wait()
-
-    def place(r, _):
-        i = order[r]
+
+    def place(i, _):
         src = pl.multiple_of((i % 2) * PART, PART)
-        dst = pl.multiple_of(r * PART, PART)
+        dst = pl.multiple_of(rank[i] * PART, PART)
         ks[pl.ds(dst, PART), :] = kall[i // 2, pl.ds(src, PART), :]
         vs[pl.ds(dst, PART), :] = kall[i // 2, pl.ds(src + 2 * PART, PART), :]
         return 0
 
-    lax.fori_loop(0, BLOCKS, place, 0, unroll=8)
+    for c in range(4):
+        key_copies[c].wait()
+        lax.fori_loop(16 * c, 16 * c + 16, place, 0, unroll=8)
     for j in range(KEYS // CHUNK):
         span = slice(j * CHUNK, (j + 1) * CHUNK)
         kst[:, span] = ks[span, :].T
@@ -213,14 +210,19 @@
             dq[hb4] += dot(kst[:, span], dlow, NN)
 
         def body(j, _):
-            step(2 * j, SPAN, False)
-            step(2 * j + 1, SPAN, False)
+            for k in range(3):
+                step(3 * j + k, SPAN, False)
             return 0
 
-        lax.fori_loop(0, full // 2, body, 0)
-
-        @pl.when(full % 2 == 1)
+        lax.fori_loop(0, full // 3, body, 0)
+
+        @pl.when(full % 3 == 1)
         def _():
+            step(full - 1, SPAN, False)
+
+        @pl.when(full % 3 == 2)
+        def _():
+            step(full - 2, SPAN, False)
             step(full - 1, SPAN, False)
 
         @pl.when(rest > SPAN // 2)
@@ -296,7 +298,6 @@
             pltpu.VMEM((8, QROWS, DH), jnp.bfloat16),
             pltpu.VMEM((SHARDS, KROWS, DH), jnp.bfloat16),
             pltpu.VMEM((SHARDS, 4 * PART, DH), jnp.bfloat16),
-            pltpu.SMEM((2 * BLOCKS,), jnp.int32),
             pltpu.SMEM((2 * BLOCKS,), jnp.int32),
             pltpu.SMEM((2 * BLOCKS,), jnp.int32),
             pltpu.SMEM((2 * BLOCKS,), jnp.int32),

time: 102 us -> 101 us (level)
  no operation moved by 1% of the time
where the time goes in v4:
time: 101 us; the launch traced here: 100 us
  starting transfers between devices  36.7 us (36%)
  waiting for transfers between devices  27.3 us (27%)
  Pallas kernels  21.9 us (22%)
  blocking collectives  8.21 us (8%)
  local copies, waits for them, and re-layouts  4.27 us (4%)
    pallas_call x1, Pallas kernels, tile(): pl.pallas_call(tile_kernel, out_shape=(jax.ShapeDtypeStruct((4, 2, DH, 2...  16.9 us
    all_to_all x1, waiting for transfers between devices, shards(): dkv = lax.all_to_all(dkv, KEY_GROUP, 0, 0, tiled=True)  10 us
    all_to_all x1, starting transfers between devices, shards(): column = lax.all_to_all(kmsg, 'z', 0, 0, tiled=True)  9.03 us
    all_gather x1, blocking collectives, shards(): quarters = lax.all_gather(mine, HEADS, tiled=False)  8.21 us
    ppermute x3, waiting for transfers between devices, shards(): dq = dq + lax.ppermute(low[i + 1], axes, route).astype(jnp.float32)  8.16 us
    ppermute x4, starting transfers between devices, shards(): far = [lax.ppermute(message, 'core', SWAP) for message in near]  7.27 us
    all_to_all x1, starting transfers between devices, shards(): dkv = lax.all_to_all(dkv, KEY_GROUP, 0, 0, tiled=True)  5.34 us
    all_to_all x1, waiting for transfers between devices, shards(): column = lax.all_to_all(kmsg, 'z', 0, 0, tiled=True)  5.2 us
  transfers between devices with their start and end apart: 16, of which 8 were waited for; matrix products, arithmetic and copies ran while one was open for 2% of the time, Pallas kernels for 3%

profile of v4, /device:TPU:1, one launch (start us, length us, event | category | flops | bytes accessed | tf_op | source)
XLA Modules:
  0.0 100.2 jit_solution(10426503313990228165)
XLA Ops:
  0.6 0.0 copy-start.2
  0.6 2.4 %pack.2 = bf16[8,136,128]{2,1,0:T(8,128)(2,1)} custom-call(s32[2]{0:T(128)} %block_pos.3, bf16[256,128]{1,0:T(8,128)(2,1)} %key_in.1, bf16[256,128]{1,0:T(8,128)(2,1)} %value_in.1), custom_call_target="tpu_custom_call" | custom-call | tf_op jit(solution)/shard_map/pack/pallas_call | solution.py:275
  3.1 9.0 %all-to-all-start = ((bf16[8,136,128]{2,1,0:T(8,128)(2,1)}), bf16[8,136,128]{2,1,0:T(8,128)(2,1)S(1)}, u32[]{:S(2)}, u32[]{:S(2)}) async-start(bf16[8,136,128]{2,1,0:T(8,128)(2,1)} %pack.2), calls=%async_computation | async-start | bytes 557056 | tf_op jit(solution)/shard_map/all_to_all | solution.py:330
  12.1 2.6 %pack.3.refs_0_ = bf16[1056,128]{1,0:T(8,128)(2,1)} custom-call(s32[2]{0:T(128)} %block_pos.3, bf16[256,256]{1,0:T(8,128)(2,1)} %refs_0_.1, bf16[256,256]{1,0:T(8,128)(2,1)} %refs_1_.1, bf16[256,256]{1,0:T(8,128)(2,1)} %refs_2_.1, f32[2,256]{1,0:T(2,128)} %refs_3_.1), custom_call_target="tpu_custom_call" | custom-call | tf_op jit(solution)/shard_map/pack/pallas_call | solution.py:275
  14.7 3.0 %collective-permute-start.3 = (bf16[1056,128]{1,0:T(8,128)(2,1)}, bf16[1056,128]{1,0:T(8,128)(2,1)S(1)}, u32[]{:S(2)}, u32[]{:S(2)}) collective-permute-start(bf16[1056,128]{1,0:T(8,128)(2,1)} %pack.3.refs_0_), channel_id=1, source_target_pairs={{0,4},{4,0},{1,5},{5,1},{2,6},{6,2},{3,7},{7,3},{8,12},{12,8},{9,1... | collective-permute-start | bytes 811016 | tf_op jit(solution)/shard_map/ppermute | solution.py:331
  17.7 0.0 copy-done.2
  17.7 5.2 %all-to-all-done.refs_8_ = bf16[8,136,128]{2,1,0:T(8,128)(2,1)S(1)} async-done(((bf16[8,136,128]{2,1,0:T(8,128)(2,1)}), bf16[8,136,128]{2,1,0:T(8,128)(2,1)S(1)}, u32[]{:S(2)}, u32[]{:S(2)}) %all-to-all-start) | async-done | bytes 278560 | tf_op jit(solution)/shard_map/all_to_all | solution.py:330
  22.9 2.5 %collective-permute-start = (bf16[8,136,128]{2,1,0:T(8,128)(2,1)S(1)}, bf16[8,136,128]{2,1,0:T(8,128)(2,1)S(1)}, u32[]{:S(2)}, u32[]{:S(2)}) collective-permute-start(bf16[8,136,128]{2,1,0:T(8,128)(2,1)S(1)} %all-to-all-done.refs_8_), channel_id=1, source_target_pairs={{0,24},{8,0},{16,8},{24,16},{1,25},{9,1},{17,9},{25,17},{2,26},{10... | collective-permute-start | bytes 835592 | tf_op jit(solution)/shard_map/ppermute | solution.py:333
  25.4 0.5 collective-permute-start.1
  25.9 1.3 %collective-permute-start.4 = (bf16[1056,128]{1,0:T(8,128)(2,1)}, bf16[1056,128]{1,0:T(8,128)(2,1)S(1)}, u32[]{:S(2)}, u32[]{:S(2)}) collective-permute-start(bf16[1056,128]{1,0:T(8,128)(2,1)} %pack.3.refs_0_), channel_id=1, source_target_pairs={{0,2},{2,0},{1,3},{3,1},{4,6},{6,4},{5,7},{7,5},{8,10},{10,8},{9,1... | collective-permute-start | bytes 811016 | tf_op jit(solution)/shard_map/ppermute | solution.py:335
  27.2 1.9 %collective-permute-start.5 = (bf16[1056,128]{1,0:T(8,128)(2,1)}, bf16[1056,128]{1,0:T(8,128)(2,1)S(1)}, u32[]{:S(2)}, u32[]{:S(2)}) collective-permute-start(bf16[1056,128]{1,0:T(8,128)(2,1)} %pack.3.refs_0_), channel_id=1, source_target_pairs={{0,6},{2,4},{4,2},{6,0},{1,7},{3,5},{5,3},{7,1},{8,14},{10,12},{12... | collective-permute-start | bytes 811016 | tf_op jit(solution)/shard_map/ppermute | solution.py:335
  29.1 0.0 collective-permute-done.3.refs_2_
  29.1 0.6 collective-permute-start.2
  29.7 0.1 reshape_squeeze.12
  29.8 1.9 %collective-permute-done.4.refs_1_ = bf16[1056,128]{1,0:T(8,128)(2,1)S(1)} collective-permute-done((bf16[1056,128]{1,0:T(8,128)(2,1)}, bf16[1056,128]{1,0:T(8,128)(2,1)S(1)}, u32[]{:S(2)}, u32[]{:S(2)}) %collective-permute-start.4) | collective-permute-done | bytes 270368 | tf_op jit(solution)/shard_map/ppermute | solution.py:335
  31.7 3.8 %collective-permute-start.8 = (bf16[1056,128]{1,0:T(8,128)(2,1)S(1)}, bf16[1056,128]{1,0:T(8,128)(2,1)S(1)}, u32[]{:S(2)}, u32[]{:S(2)}) collective-permute-start(bf16[1056,128]{1,0:T(8,128)(2,1)S(1)} %collective-permute-done.3.refs_2_), channel_id=1, source_target_pairs={{0,1},{1,0},{2,3},{3,2},{4,5},{5,4},{6,7},{7,6},{8,9},{9,8},{10,11... | collective-permute-start | bytes 811016 | tf_op jit(solution)/shard_map/ppermute | solution.py:336
  35.5 0.0 collective-permute-done.5.refs_3_
  35.5 2.8 %collective-permute-start.6 = (bf16[1056,128]{1,0:T(8,128)(2,1)}, bf16[1056,128]{1,0:T(8,128)(2,1)S(1)}, u32[]{:S(2)}, u32[]{:S(2)}) collective-permute-start(bf16[1056,128]{1,0:T(8,128)(2,1)} %pack.3.refs_0_), channel_id=1, source_target_pairs={{0,1},{1,0},{2,3},{3,2},{4,5},{5,4},{6,7},{7,6},{8,9},{9,8},{10,11... | collective-permute-start | bytes 811016 | tf_op jit(solution)/shard_map/ppermute | solution.py:336
  38.3 0.0 collective-permute-done.refs_9_
  38.3 0.1 collective-permute-start.7
  38.4 0.0 collective-permute-done.1.refs_10_
  38.4 0.6 collective-permute-start.9
  39.0 0.1 reshape_squeeze.13
  39.1 0.1 reshape_squeeze.14
  39.2 0.5 collective-permute-done.2.refs_11_
  39.8 0.1 reshape_squeeze.15
  39.8 0.1 concatenate.3
  39.9 0.5 convert_element_type.47.info
  40.5 0.0 collective-permute-done.8.refs_6_
  40.5 0.0 collective-permute-done.6.refs_4_
  40.5 0.0 copy-start.11
  40.5 0.0 collective-permute-done.7.refs_5_
  40.5 0.0 copy-start.12
  40.5 0.0 collective-permute-done.9.refs_7_
  40.5 0.0 copy-done.1
  40.5 0.0 copy-done.7
  40.5 0.0 copy-done.8
  40.5 0.0 copy-done.9
  40.6 0.0 copy-done.3
  40.6 0.0 copy-done.4
  40.6 0.6 copy-done.10
  41.2 0.1 copy-done.11
  41.3 0.1 copy-done.12
  41.4 0.7 copy-done.13
  42.1 16.9 %tile.1 = (f32[4,2,128,256]{3,2,1,0:T(8,128)}, bf16[4,2,128,256]{3,2,1,0:T(8,128)(2,1)}, bf16[8,4,128,128]{3,2,1,0:T(8,128)(2,1)}) custom-call(s32[68]{0:T(128)} %convert_element_type.47.info, bf16[1056,128]{1,0:T(8,128)(2,1)} %pack.3.refs_0_, bf16[1056,128]{1,0:T(8,128)(2,1)} %copy-done.8, bf16[1056,128]{1,0:T(8,128)(2,1)} %copy-done.7, ...), custom_call_target="tpu_custom_call" | custom-call | flops 6000000000 | bytes 6291456 | tf_op jit(solution)/shard_map/tile/pallas_call | solution.py:288
  59.1 5.3 %all-to-all-start.1 = ((bf16[32,128,128]{2,1,0:T(8,128)(2,1)}), bf16[32,128,128]{2,1,0:T(8,128)(2,1)S(1)}, u32[]{:S(2)}, u32[]{:S(2)}) async-start(bf16[32,128,128]{2,1,0:T(8,128)(2,1)} %bitcast.36), calls=%async_computation.1 | async-start | bytes 2097152 | tf_op jit(solution)/shard_map/all_to_all | solution.py:349
  64.4 1.3 %collective-permute-start.10 = (bf16[4,2,128,256]{3,2,1,0:T(8,128)(2,1)S(1)}, bf16[4,2,128,256]{3,2,1,0:T(8,128)(2,1)S(1)}, u32[]{:S(2)}, u32[]{:S(2)}) collective-permute-start(bf16[4,2,128,256]{3,2,1,0:T(8,128)(2,1)S(1)} %copy-done.6), channel_id=1, source_target_pairs={{0,1},{1,0},{2,3},{3,2},{4,5},{5,4},{6,7},{7,6},{8,9},{9,8},{10,11... | collective-permute-start | bytes 1572872 | tf_op jit(solution)/shard_map/ppermute | solution.py:343
  65.7 1.5 %collective-permute-done.10 = bf16[4,2,128,256]{3,2,1,0:T(8,128)(2,1)S(1)} collective-permute-done((bf16[4,2,128,256]{3,2,1,0:T(8,128)(2,1)S(1)}, bf16[4,2,128,256]{3,2,1,0:T(8,128)(2,1)S(1)}, u32[]{:S(2)}, u32[]{:S(2)}) %collective-permute-start.10) | collective-permute-done | bytes 524320 | tf_op jit(solution)/shard_map/ppermute | solution.py:343
  67.2 0.2 fusion.6
  67.4 1.1 %collective-permute-start.11 = (bf16[2,128,256]{2,1,0:T(8,128)(2,1)S(1)}, bf16[2,128,256]{2,1,0:T(8,128)(2,1)S(1)}, u32[]{:S(2)}, u32[]{:S(2)}) collective-permute-start(bf16[2,128,256]{2,1,0:T(8,128)(2,1)S(1)} %get-tuple-element.15), channel_id=1, source_target_pairs={{0,2},{2,0},{1,3},{3,1},{4,6},{6,4},{5,7},{7,5},{8,10},{10,8},{9,1... | collective-permute-start | bytes 393224 | tf_op jit(solution)/shard_map/ppermute | solution.py:347
  68.5 2.4 %collective-permute-start.12 = (bf16[2,128,256]{2,1,0:T(8,128)(2,1)S(1)}, bf16[2,128,256]{2,1,0:T(8,128)(2,1)S(1)}, u32[]{:S(2)}, u32[]{:S(2)}) collective-permute-start(bf16[2,128,256]{2,1,0:T(8,128)(2,1)S(1)} %get-tuple-element.17), channel_id=1, source_target_pairs={{0,4},{4,0},{1,5},{5,1},{2,6},{6,2},{3,7},{7,3},{8,12},{12,8},{9,1... | collective-permute-start | bytes 393224 | tf_op jit(solution)/shard_map/ppermute | solution.py:347
  70.9 0.4 collective-permute-start.13
  71.4 0.8 collective-permute-done.11
  72.2 4.8 %collective-permute-done.12 = bf16[2,128,256]{2,1,0:T(8,128)(2,1)S(1)} collective-permute-done((bf16[2,128,256]{2,1,0:T(8,128)(2,1)S(1)}, bf16[2,128,256]{2,1,0:T(8,128)(2,1)S(1)}, u32[]{:S(2)}, u32[]{:S(2)}) %collective-permute-start.12) | collective-permute-done | bytes 131104 | tf_op jit(solution)/shard_map/ppermute | solution.py:347
  77.0 2.5 %collective-permute-done.13 = bf16[2,128,256]{2,1,0:T(8,128)(2,1)S(1)} collective-permute-done((bf16[2,128,256]{2,1,0:T(8,128)(2,1)S(1)}, bf16[2,128,256]{2,1,0:T(8,128)(2,1)S(1)}, u32[]{:S(2)}, u32[]{:S(2)}) %collective-permute-start.13) | collective-permute-done | bytes 131104 | tf_op jit(solution)/shard_map/ppermute | solution.py:347
  79.5 0.1 fusion.4
  79.6 0.1 copy.15
  79.8 0.7 copy.20
  80.4 10.0 %all-to-all-done.1 = bf16[32,128,128]{2,1,0:T(8,128)(2,1)S(1)} async-done(((bf16[32,128,128]{2,1,0:T(8,128)(2,1)}), bf16[32,128,128]{2,1,0:T(8,128)(2,1)S(1)}, u32[]{:S(2)}, u32[]{:S(2)}) %all-to-all-start.1) | async-done | bytes 1048608 | tf_op jit(solution)/shard_map/all_to_all | solution.py:349
  90.5 0.2 convert_reduce_fusion
  90.6 0.1 fusion.5
  90.7 8.2 %all_gather.4 = bf16[4,128,128]{2,1,0:T(8,128)(2,1)S(1)} all-gather(bf16[1,128,128]{2,1,0:T(8,128)(2,1)S(1)} %fusion.5), channel_id=1, replica_groups=mesh['z'=8,'x'=4,'yh'=2,'yl'=2,'core'=2] {'yl','core'}, dimensions={0}, use_global_device_ids=true | all-gather | bytes 163840 | tf_op jit(solution)/shard_map/all_gather | solution.py:353
  98.9 0.6 copy.16
  99.5 0.6 copy.17
  (24 shorter events, 0.2 us)
Async XLA Ops:
  0.6 17.1 %copy-start.2 = (s32[2]{0:T(128)S(1)}, s32[2]{0:T(128)}, u32[]{:S(2)}) copy-start(s32[2]{0:T(128)} %block_pos.3) | copy-start | bytes 28
  3.1 19.8 %all-to-all-start = ((bf16[8,136,128]{2,1,0:T(8,128)(2,1)}), bf16[8,136,128]{2,1,0:T(8,128)(2,1)S(1)}, u32[]{:S(2)}, u32[]{:S(2)}) async-start(bf16[8,136,128]{2,1,0:T(8,128)(2,1)} %pack.2), calls=%async_computation | async-start | bytes 557056 | tf_op jit(solution)/shard_map/all_to_all | solution.py:330
  14.7 14.4 %collective-permute-start.3 = (bf16[1056,128]{1,0:T(8,128)(2,1)}, bf16[1056,128]{1,0:T(8,128)(2,1)S(1)}, u32[]{:S(2)}, u32[]{:S(2)}) collective-permute-start(bf16[1056,128]{1,0:T(8,128)(2,1)} %pack.3.refs_0_), channel_id=1, source_target_pairs={{0,4},{4,0},{1,5},{5,1},{2,6},{6,2},{3,7},{7,3},{8,12},{12,8},{9,1... | collective-permute-start | bytes 811016 | tf_op jit(solution)/shard_map/ppermute | solution.py:331
  22.9 17.6 %copy-start.1 = (bf16[8,136,128]{2,1,0:T(8,128)(2,1)}, bf16[8,136,128]{2,1,0:T(8,128)(2,1)S(1)}, u32[]{:S(2)}) copy-start(bf16[8,136,128]{2,1,0:T(8,128)(2,1)S(1)} %all-to-all-done.refs_8_) | copy-start | bytes 835588
  22.9 15.4 %collective-permute-start = (bf16[8,136,128]{2,1,0:T(8,128)(2,1)S(1)}, bf16[8,136,128]{2,1,0:T(8,128)(2,1)S(1)}, u32[]{:S(2)}, u32[]{:S(2)}) collective-permute-start(bf16[8,136,128]{2,1,0:T(8,128)(2,1)S(1)} %all-to-all-done.refs_8_), channel_id=1, source_target_pairs={{0,24},{8,0},{16,8},{24,16},{1,25},{9,1},{17,9},{25,17},{2,26},{10... | collective-permute-start | bytes 835592 | tf_op jit(solution)/shard_map/ppermute | solution.py:333
  25.4 13.0 %collective-permute-start.1 = (bf16[8,136,128]{2,1,0:T(8,128)(2,1)S(1)}, bf16[8,136,128]{2,1,0:T(8,128)(2,1)S(1)}, u32[]{:S(2)}, u32[]{:S(2)}) collective-permute-start(bf16[8,136,128]{2,1,0:T(8,128)(2,1)S(1)} %all-to-all-done.refs_8_), channel_id=1, source_target_pairs={{0,16},{8,24},{16,0},{24,8},{1,17},{9,25},{17,1},{25,9},{2,18},{10... | collective-permute-start | bytes 835592 | tf_op jit(solution)/shard_map/ppermute | solution.py:333
  25.9 5.8 %collective-permute-start.4 = (bf16[1056,128]{1,0:T(8,128)(2,1)}, bf16[1056,128]{1,0:T(8,128)(2,1)S(1)}, u32[]{:S(2)}, u32[]{:S(2)}) collective-permute-start(bf16[1056,128]{1,0:T(8,128)(2,1)} %pack.3.refs_0_), channel_id=1, source_target_pairs={{0,2},{2,0},{1,3},{3,1},{4,6},{6,4},{5,7},{7,5},{8,10},{10,8},{9,1... | collective-permute-start | bytes 811016 | tf_op jit(solution)/shard_map/ppermute | solution.py:335
  27.2 8.3 %collective-permute-start.5 = (bf16[1056,128]{1,0:T(8,128)(2,1)}, bf16[1056,128]{1,0:T(8,128)(2,1)S(1)}, u32[]{:S(2)}, u32[]{:S(2)}) collective-permute-start(bf16[1056,128]{1,0:T(8,128)(2,1)} %pack.3.refs_0_), channel_id=1, source_target_pairs={{0,6},{2,4},{4,2},{6,0},{1,7},{3,5},{5,3},{7,1},{8,14},{10,12},{12... | collective-permute-start | bytes 811016 | tf_op jit(solution)/shard_map/ppermute | solution.py:335
  29.1 11.4 %copy-start.7 = (bf16[1056,128]{1,0:T(8,128)(2,1)}, bf16[1056,128]{1,0:T(8,128)(2,1)S(1)}, u32[]{:S(2)}) copy-start(bf16[1056,128]{1,0:T(8,128)(2,1)S(1)} %collective-permute-done.3.refs_2_) | copy-start | bytes 811012
  29.1 10.6 %collective-permute-start.2 = (bf16[8,136,128]{2,1,0:T(8,128)(2,1)S(1)}, bf16[8,136,128]{2,1,0:T(8,128)(2,1)S(1)}, u32[]{:S(2)}, u32[]{:S(2)}) collective-permute-start(bf16[8,136,128]{2,1,0:T(8,128)(2,1)S(1)} %all-to-all-done.refs_8_), channel_id=1, source_target_pairs={{0,8},{8,16},{16,24},{24,0},{1,9},{9,17},{17,25},{25,1},{2,10},{10... | collective-permute-start | bytes 835592 | tf_op jit(solution)/shard_map/ppermute | solution.py:333
  31.7 8.8 %copy-start.8 = (bf16[1056,128]{1,0:T(8,128)(2,1)}, bf16[1056,128]{1,0:T(8,128)(2,1)S(1)}, u32[]{:S(2)}) copy-start(bf16[1056,128]{1,0:T(8,128)(2,1)S(1)} %collective-permute-done.4.refs_1_) | copy-start | bytes 811012
  31.7 8.8 %collective-permute-start.8 = (bf16[1056,128]{1,0:T(8,128)(2,1)S(1)}, bf16[1056,128]{1,0:T(8,128)(2,1)S(1)}, u32[]{:S(2)}, u32[]{:S(2)}) collective-permute-start(bf16[1056,128]{1,0:T(8,128)(2,1)S(1)} %collective-permute-done.3.refs_2_), channel_id=1, source_target_pairs={{0,1},{1,0},{2,3},{3,2},{4,5},{5,4},{6,7},{7,6},{8,9},{9,8},{10,11... | collective-permute-start | bytes 811016 | tf_op jit(solution)/shard_map/ppermute | solution.py:336
  35.5 5.0 %copy-start.9 = (bf16[1056,128]{1,0:T(8,128)(2,1)}, bf16[1056,128]{1,0:T(8,128)(2,1)S(1)}, u32[]{:S(2)}) copy-start(bf16[1056,128]{1,0:T(8,128)(2,1)S(1)} %collective-permute-done.5.refs_3_) | copy-start | bytes 811012
  35.5 5.0 %collective-permute-start.6 = (bf16[1056,128]{1,0:T(8,128)(2,1)}, bf16[1056,128]{1,0:T(8,128)(2,1)S(1)}, u32[]{:S(2)}, u32[]{:S(2)}) collective-permute-start(bf16[1056,128]{1,0:T(8,128)(2,1)} %pack.3.refs_0_), channel_id=1, source_target_pairs={{0,1},{1,0},{2,3},{3,2},{4,5},{5,4},{6,7},{7,6},{8,9},{9,8},{10,11... | collective-permute-start | bytes 811016 | tf_op jit(solution)/shard_map/ppermute | solution.py:336
  38.3 2.3 %copy-start.3 = (bf16[8,136,128]{2,1,0:T(8,128)(2,1)}, bf16[8,136,128]{2,1,0:T(8,128)(2,1)S(1)}, u32[]{:S(2)}) copy-start(bf16[8,136,128]{2,1,0:T(8,128)(2,1)S(1)} %collective-permute-done.refs_9_) | copy-start | bytes 835588
  38.3 2.2 %collective-permute-start.7 = (bf16[1056,128]{1,0:T(8,128)(2,1)S(1)}, bf16[1056,128]{1,0:T(8,128)(2,1)S(1)}, u32[]{:S(2)}, u32[]{:S(2)}) collective-permute-start(bf16[1056,128]{1,0:T(8,128)(2,1)S(1)} %collective-permute-done.4.refs_1_), channel_id=1, source_target_pairs={{0,1},{1,0},{2,3},{3,2},{4,5},{5,4},{6,7},{7,6},{8,9},{9,8},{10,11... | collective-permute-start | bytes 811016 | tf_op jit(solution)/shard_map/ppermute | solution.py:336
  38.4 2.2 %copy-start.4 = (bf16[8,136,128]{2,1,0:T(8,128)(2,1)}, bf16[8,136,128]{2,1,0:T(8,128)(2,1)S(1)}, u32[]{:S(2)}) copy-start(bf16[8,136,128]{2,1,0:T(8,128)(2,1)S(1)} %collective-permute-done.1.refs_10_) | copy-start | bytes 835588
  38.4 2.1 %collective-permute-start.9 = (bf16[1056,128]{1,0:T(8,128)(2,1)S(1)}, bf16[1056,128]{1,0:T(8,128)(2,1)S(1)}, u32[]{:S(2)}, u32[]{:S(2)}) collective-permute-start(bf16[1056,128]{1,0:T(8,128)(2,1)S(1)} %collective-permute-done.5.refs_3_), channel_id=1, source_target_pairs={{0,1},{1,0},{2,3},{3,2},{4,5},{5,4},{6,7},{7,6},{8,9},{9,8},{10,11... | collective-permute-start | bytes 811016 | tf_op jit(solution)/shard_map/ppermute | solution.py:336
  39.7 0.9 copy-start.5
  40.5 0.7 copy-start.10
  40.5 0.8 copy-start.11
  40.5 0.9 copy-start.12
  41.4 0.7 copy-start.13
  59.0 5.4 %copy-start.6 = (bf16[4,2,128,256]{3,2,1,0:T(8,128)(2,1)S(1)}, bf16[4,2,128,256]{3,2,1,0:T(8,128)(2,1)}, u32[]{:S(2)}) copy-start(bf16[4,2,128,256]{3,2,1,0:T(8,128)(2,1)} %get-tuple-element.11) | copy-start | bytes 1572868
  59.0 8.2 %copy-start = (f32[4,2,128,256]{3,2,1,0:T(8,128)S(1)}, f32[4,2,128,256]{3,2,1,0:T(8,128)}, u32[]{:S(2)}) copy-start(f32[4,2,128,256]{3,2,1,0:T(8,128)} %get-tuple-element.10) | copy-start | bytes 3145732
  59.1 31.4 %all-to-all-start.1 = ((bf16[32,128,128]{2,1,0:T(8,128)(2,1)}), bf16[32,128,128]{2,1,0:T(8,128)(2,1)S(1)}, u32[]{:S(2)}, u32[]{:S(2)}) async-start(bf16[32,128,128]{2,1,0:T(8,128)(2,1)} %bitcast.36), calls=%async_computation.1 | async-start | bytes 2097152 | tf_op jit(solution)/shard_map/all_to_all | solution.py:349
  64.4 2.8 %collective-permute-start.10 = (bf16[4,2,128,256]{3,2,1,0:T(8,128)(2,1)S(1)}, bf16[4,2,128,256]{3,2,1,0:T(8,128)(2,1)S(1)}, u32[]{:S(2)}, u32[]{:S(2)}) collective-permute-start(bf16[4,2,128,256]{3,2,1,0:T(8,128)(2,1)S(1)} %copy-done.6), channel_id=1, source_target_pairs={{0,1},{1,0},{2,3},{3,2},{4,5},{5,4},{6,7},{7,6},{8,9},{9,8},{10,11... | collective-permute-start | bytes 1572872 | tf_op jit(solution)/shard_map/ppermute | solution.py:343
  67.4 4.8 %collective-permute-start.11 = (bf16[2,128,256]{2,1,0:T(8,128)(2,1)S(1)}, bf16[2,128,256]{2,1,0:T(8,128)(2,1)S(1)}, u32[]{:S(2)}, u32[]{:S(2)}) collective-permute-start(bf16[2,128,256]{2,1,0:T(8,128)(2,1)S(1)} %get-tuple-element.15), channel_id=1, source_target_pairs={{0,2},{2,0},{1,3},{3,1},{4,6},{6,4},{5,7},{7,5},{8,10},{10,8},{9,1... | collective-permute-start | bytes 393224 | tf_op jit(solution)/shard_map/ppermute | solution.py:347
  68.5 8.5 %collective-permute-start.12 = (bf16[2,128,256]{2,1,0:T(8,128)(2,1)S(1)}, bf16[2,128,256]{2,1,0:T(8,128)(2,1)S(1)}, u32[]{:S(2)}, u32[]{:S(2)}) collective-permute-start(bf16[2,128,256]{2,1,0:T(8,128)(2,1)S(1)} %get-tuple-element.17), channel_id=1, source_target_pairs={{0,4},{4,0},{1,5},{5,1},{2,6},{6,2},{3,7},{7,3},{8,12},{12,8},{9,1... | collective-permute-start | bytes 393224 | tf_op jit(solution)/shard_map/ppermute | solution.py:347
  70.9 8.6 %collective-permute-start.13 = (bf16[2,128,256]{2,1,0:T(8,128)(2,1)S(1)}, bf16[2,128,256]{2,1,0:T(8,128)(2,1)S(1)}, u32[]{:S(2)}, u32[]{:S(2)}) collective-permute-start(bf16[2,128,256]{2,1,0:T(8,128)(2,1)S(1)} %get-tuple-element.16), channel_id=1, source_target_pairs={{0,6},{2,4},{4,2},{6,0},{1,7},{3,5},{5,3},{7,1},{8,14},{10,12},{12... | collective-permute-start | bytes 393224 | tf_op jit(solution)/shard_map/ppermute | solution.py:347
